TPU v7x, 32 devices: a whole 2x2x4 slice. The times are simulated.
32 devices in a mesh: dom: 8 (over z, x), grid: 4 (over y, core).
Axes of the slice: x: 2, y: 2, z: 4, core: 2. Of those that a mesh axis runs over, the one named last changes fastest.
Arguments:
- adjoint: float32 [4, 6, 1024, 128], P('grid', None, 'dom'), may hold values from -6 to 6
- jac_diag: float32 [4, 6, 6, 1024, 128], P('grid', None, None, 'dom'), may hold values from -6 to 6
- jac_face: float32 [4, 6, 4, 6, 1024, 128], P('grid', None, None, None, 'dom'), may hold values from -3 to 3
- metric: float32 [4, 6, 3, 4, 1024, 128], P('grid', None, None, None, 'dom'), may hold values from -1.5 to 1.5
- node_id: int32 [4, 4, 1024, 128], P('grid', None, 'dom'), may hold values from 0 to 16383
- fringe_cell: int32 [32, 32, 128], P(('dom', 'grid')), may hold values from 0 to 16383
- donor_cell: int32 [32, 32, 128], P(('dom', 'grid')), may hold values from 0 to 16383
- fringe_weight: float32 [32, 32, 128], P(('dom', 'grid')), may hold values from 0.05 to 1
- donor_count: int32 [32, 32], P(('dom', 'grid')), may hold values from 16 to 128, as said below
Outputs:
- product: float32 [4, 6, 1024, 128], P('grid', None, 'dom')
- node_sens: float32 [3, 16384], P(None, ('dom', 'grid'))
Inputs may be any that keep to these rules, and one draw needn't show every extreme that they name: The live slots from p to q are slots 0 to donor_count[q, p] - 1; in every draw some receiving device has 128 live slots from every sender.
All inputs are finite; a program needn't handle non-finite values.
Results may differ from a plain program's by a relative error of at most 0.000071.
Values sent between devices are 32-bit elements; how exact they have to be, the bound alone decides.
No kernel may reach another device: no remote copies, remote signals or barrier semaphores. Data moves between devices by JAX's collectives and lax.ppermute only.
A program may use at most 192 MiB of HBM per device.

v0:
```python
import jax
import jax.numpy as jnp
from jax import lax
from jax.sharding import PartitionSpec as P

NODE_DEV = 512


def shifted(block, axis, distance):
    devices = range(lax.axis_size(axis))
    route = [(i - distance, i) for i in devices if i - distance in devices]
    return lax.ppermute(block, axis, route)


def contract(blocks, adjoint_local):
    running = blocks[0] * adjoint_local[0]
    for variable in range(1, adjoint_local.shape[0]):
        running = running + blocks[variable] * adjoint_local[variable]
    return running


def local(
    adjoint,
    jac_diag,
    jac_face,
    metric,
    node_id,
    fringe_cell,
    donor_cell,
    fringe_weight,
    donor_count,
):
    values = adjoint[0]
    variables, row_count, block_width = values.shape
    diagonal_part = contract(jac_diag[0], values)
    face_terms = contract(jac_face[0], values)
    corner_terms = contract(metric[0], values)
    from_below = shifted(face_terms[0, :, 0, :], "dom", -1)
    from_above = shifted(face_terms[1, :, row_count - 1, :], "dom", 1)
    carried = jnp.concatenate([face_terms[0, :, 1:, :], from_below[:, None, :]], axis=1)
    carried = carried + jnp.concatenate([from_above[:, None, :], face_terms[1, :, :-1, :]], axis=1)
    carried = carried + jnp.pad(face_terms[2, :, :, 1:], ((0, 0), (0, 0), (0, 1)))
    carried = carried + jnp.pad(face_terms[3, :, :, :-1], ((0, 0), (0, 0), (1, 0)))
    flat_values = values.reshape(variables, row_count * block_width)
    payload = jnp.take(flat_values, fringe_cell[0], axis=1)
    capacity = payload.shape[2]
    received = lax.all_to_all(payload, ("dom", "grid"), split_axis=1, concat_axis=1, tiled=True)
    live_slots = jnp.arange(capacity, dtype=jnp.int32)[None, :] < donor_count[0][:, None]
    slot_weights = jnp.where(live_slots, fringe_weight[0], jnp.zeros_like(fringe_weight[0]))
    interp = jnp.zeros((variables, row_count * block_width), jnp.float32)
    interp = interp.at[:, donor_cell[0]].add(-(received * slot_weights[None]))
    product = diagonal_part + carried + interp.reshape(variables, row_count, block_width)
    node_total = NODE_DEV * lax.axis_size("dom") * lax.axis_size("grid")
    partial_value = (
        jnp.zeros((corner_terms.shape[0], node_total), jnp.float32)
        .at[:, node_id[0]]
        .add(corner_terms)
    )
    node_sens = lax.psum_scatter(partial_value, ("dom", "grid"), scatter_dimension=1, tiled=True)
    return (product[None], node_sens)


def solution(mesh):
    in_specs = (
        P("grid", None, "dom", None),
        P("grid", None, None, "dom", None),
        P("grid", None, None, None, "dom", None),
        P("grid", None, None, None, "dom", None),
        P("grid", None, "dom", None),
        P(("dom", "grid"), None, None),
        P(("dom", "grid"), None, None),
        P(("dom", "grid"), None, None),
        P(("dom", "grid"), None),
    )
    out_specs = (P("grid", None, "dom", None), P(None, ("dom", "grid")))
    return jax.shard_map(local, mesh=mesh, in_specs=in_specs, out_specs=out_specs, check_vma=False)
```

profile of v0, /device:TPU:0, one launch (start us, length us, event | category | flops | bytes accessed | tf_op | source)
XLA Modules:
  0.0 581.0 jit_solution(3592271948561429197)
XLA Ops:
  7.2 1.0 slice_bitcast_fusion.9
  8.2 0.0 copy-start.2
  8.2 0.0 copy-start
  8.2 5.0 fusion.4
  13.2 1.3 collective-permute-start
  14.5 5.5 collective-permute-start.1
  20.1 4.7 copy.26
  24.8 17.6 %gather_fusion = f32[4096,6]{1,0:T(8,128)} fusion(f32[6,16384]{0,1:T(8,128)} %bitcast.162, s32[4096]{0:T(1024)S(1)} %fusion.27), kind=kCustom, calls=%fused_computation | custom fusion | bytes 212992 | tf_op jit(solution)/shard_map/jit(_take)/gather | solution.py:45
  42.4 2.2 copy.27
  44.6 0.7 select_bitcast_fusion
  45.3 6.4 %all-to-all-start = ((f32[6,32,128]{2,0,1:T(8,128)}), f32[6,32,128]{2,0,1:T(8,128)}, u32[]{:S(2)}, u32[]{:S(2)}) async-start(f32[6,32,128]{2,0,1:T(8,128)} %select_bitcast_fusion), calls=%async_computation | async-start | bytes 262144 | tf_op jit(solution)/shard_map/all_to_all | solution.py:47
  51.7 0.0 reduce-scatter.2.cloned.1.call-start
  51.8 2.8 fusion.10
  54.5 16.5 %copy.32 = f32[4,128,128,3]{3,2,1,0:T(8,128)} copy(f32[4,128,128,3]{2,1,0,3:T(8,128)S(1)} %fusion.10) | data formatting | bytes 1572864 | tf_op jit(solution)/shard_map/add | solution.py:18
  71.0 351.2 %scatter_custom_fusion.1 = f32[3,16384]{0,1:T(8,128)} fusion(s32[65536]{0:T(1024)S(1)} %bitcast.164, f32[65536,3]{1,0:T(8,128)} %bitcast.160, f32[]{:T(128)} %constant.7.clone.1), kind=kCustom, calls=%fused_computation.3 | custom fusion | flops 196608 | bytes 197120 | tf_op jit(solution)/shard_map/scatter-add | solution.py:57
  422.2 0.0 reduce-scatter.2.cloned.1.call-update
  422.2 0.0 copy-start.3
  422.2 0.0 copy-start.5
  422.2 0.0 copy-start.4
  422.2 0.1 slice_bitcast_fusion.2
  422.3 0.2 slice_bitcast_fusion.1
  422.5 0.4 copy-done.3
  422.9 0.1 select_bitcast_fusion.1
  423.0 0.0 collective-permute-done.1
  423.0 0.0 all-to-all-done
  423.1 0.9 negate_bitcast_fusion
  424.0 2.0 copy.28
  426.0 26.4 %scatter_custom_fusion = f32[6,16384]{0,1:T(8,128)} fusion(s32[4096]{0:T(1024)S(1)} %fusion.25, f32[4096,6]{1,0:T(8,128)} %copy.28, f32[]{:T(128)} %constant.7.clone.1), kind=kCustom, calls=%fused_computation.5 | custom fusion | flops 24576 | bytes 393728 | tf_op jit(solution)/shard_map/scatter-add | solution.py:51
  452.4 5.3 copy.29
  457.7 2.8 fusion.19
  460.5 112.0 %reduce-scatter.2.cloned.1.call-done = f32[3,512]{0,1:T(8,128)} async-done(((f32[3,16384]{0,1:T(8,128)}), f32[3,512]{0,1:T(8,128)}) %reduce-scatter.2.cloned.1.call-update) | async-done | bytes 6160 | tf_op jit(solution)/shard_map/reduce_scatter | solution.py:59
  572.5 1.7 copy.31
  (16 shorter events, 0.1 us)
Async XLA Ops:
  8.2 11.8 %copy-start.2 = (s32[1,32,128]{2,1,0:T(8,128)S(1)}, s32[1,32,128]{2,1,0:T(8,128)}, u32[]{:S(2)}) copy-start(s32[1,32,128]{2,1,0:T(8,128)} %param.14) | copy-start | bytes 49156
  8.2 11.8 %copy-start = (f32[1,6,128,128]{3,2,1,0:T(8,128)S(1)}, f32[1,6,128,128]{3,2,1,0:T(8,128)}, u32[]{:S(2)}) copy-start(f32[1,6,128,128]{3,2,1,0:T(8,128)} %param.9) | copy-start | bytes 1179652
  13.2 409.8 %collective-permute-start = (f32[6,128]{1,0:T(8,128)S(1)}, f32[6,128]{1,0:T(8,128)S(1)}, u32[]{:S(2)}, u32[]{:S(2)}) collective-permute-start(f32[6,128]{1,0:T(8,128)S(1)} %bitcast.165), channel_id=1, source_target_pairs={{4,0},{8,4},{12,8},{16,12},{20,16},{24,20},{28,24},{5,1},{9,5},{13... | collective-permute-start | bytes 9224 | tf_op jit(solution)/shard_map/ppermute | solution.py:12
  14.5 408.5 %collective-permute-start.1 = (f32[6,128]{1,0:T(8,128)S(1)}, f32[6,128]{1,0:T(8,128)S(1)}, u32[]{:S(2)}, u32[]{:S(2)}) collective-permute-start(f32[6,128]{1,0:T(8,128)S(1)} %bitcast.166), channel_id=1, source_target_pairs={{0,4},{4,8},{8,12},{12,16},{16,20},{20,24},{24,28},{1,5},{5,9},{9,... | collective-permute-start | bytes 9224 | tf_op jit(solution)/shard_map/ppermute | solution.py:12
  24.8 26.9 %copy-start.1 = (s32[1,4,128,128]{3,2,1,0:T(8,128)S(1)}, s32[1,4,128,128]{3,2,1,0:T(8,128)}, u32[]{:S(2)}) copy-start(s32[1,4,128,128]{3,2,1,0:T(8,128)} %param.13) | copy-start | bytes 786436
  45.3 377.8 %all-to-all-start = ((f32[6,32,128]{2,0,1:T(8,128)}), f32[6,32,128]{2,0,1:T(8,128)}, u32[]{:S(2)}, u32[]{:S(2)}) async-start(f32[6,32,128]{2,0,1:T(8,128)} %select_bitcast_fusion), calls=%async_computation | async-start | bytes 262144 | tf_op jit(solution)/shard_map/all_to_all | solution.py:47
  51.7 520.9 %reduce-scatter.2.cloned.1.call-start = ((), (), s32[]{:S(2)}) async-start(), calls=%async_computation.2 | async-start | bytes 8650752 | tf_op jit(solution)/shard_map/reduce_scatter | solution.py:59
  422.2 0.7 copy-start.3
  422.2 0.7 copy-start.5
  422.2 0.8 copy-start.4
Sparse Core Ops, SparseCore 0:
  422.3 150.1 reduce-scatter.1
where the time goes:
time: 582 us; the launch traced here: 581 us
  other arithmetic  390 us (67%)
  waiting for transfers between devices  112 us (19%)
  local copies, waits for them, and re-layouts  51.7 us (9%)
  between operations  14.2 us (2%)
  starting transfers between devices  13.2 us (2%)
    scatter-add x1, other arithmetic, local(): partial_value = jnp.zeros((corner_terms.shape[0], node_total), jnp.float3...  351 us
    reduce_scatter x1, waiting for transfers between devices, local(): lax.psum_scatter(partial_value, ('dom', 'grid'), scatter_dimension=1, til...  112 us
    scatter-add x1, other arithmetic, local(): interp = interp.at[:, donor_cell[0]].add(-(received * slot_weights[None]))  26.4 us
    gather x2, local copies, waits for them, and re-layouts, local(): payload = jnp.take(flat_values, fringe_cell[0], axis=1)  19.8 us
    add x1, local copies, waits for them, and re-layouts, contract(): running = running + blocks[variable] * adjoint_local[variable]  16.5 us
  transfers between devices with their start and end apart: 4, of which 1 were waited for; matrix products, arithmetic and copies ran while one was open for 75% of the time, Pallas kernels for 0%

commit v1 on v0

v1 whole, which is shorter than its diff:
```python
import functools

import jax
import jax.numpy as jnp
from jax import lax
from jax.experimental import pallas as pl
from jax.experimental.pallas import tpu as pltpu
from jax.sharding import PartitionSpec as P

NODE_DEV = 512
LANES = 128
SPAN = 256
SPAN_BITS = SPAN.bit_length() - 1
CHUNK = 32
VMEM_BYTES = 48 * 1024 * 1024
LAST_WITH_LAST = (((1,), (1,)), ((), ()))


def ceil_to(value, unit):
    return -(-value // unit) * unit


def sublane_iota(count):
    return lax.broadcasted_iota(jnp.int32, (count, LANES), 0).astype(jnp.bfloat16)


def as_code(index):
    return index.astype(jnp.float32).astype(jnp.bfloat16)


def two_parts(value):
    head = value.astype(jnp.bfloat16)
    tail = (value - head.astype(jnp.float32)).astype(jnp.bfloat16)
    return head, tail


def weighted_sum(load, adj):
    running = load(0) * adj[0]
    for variable in range(1, len(adj)):
        running = running + load(variable) * adj[variable]
    return running


def gather_and_nodes(
    place, adj_ref, metric_ref, node_ref, fringe_ref, first_ref, last_ref, out_ref, totals, split_adj
):
    step = pl.program_id(0)
    steps = pl.num_programs(0)
    variables, row_count, width = adj_ref.shape
    coords, corners, rows = metric_ref.shape[1:4]
    peers = out_ref.shape[0]
    spans = totals.shape[0] // (2 * coords)
    span_rows = SPAN // width
    node_rows = coords * NODE_DEV // width
    payload_at = node_rows
    halo_at = node_rows + variables
    zero = jnp.zeros((), jnp.bfloat16)
    one = jnp.ones((), jnp.bfloat16)

    @pl.when(step == 0)
    def _():
        head, tail = two_parts(adj_ref[...].reshape(variables * row_count, width))
        split_adj[:, :width] = head
        split_adj[:, width:] = tail
        out_ref[:, halo_at:, :] = jnp.zeros((peers, out_ref.shape[1] - halo_at, width), jnp.float32)
        top = [adj_ref[i, : first_ref.shape[3], :] for i in range(variables)]
        bottom = [adj_ref[i, row_count - last_ref.shape[3] :, :] for i in range(variables)]
        for j in range(variables):
            face_down = weighted_sum(lambda i: first_ref[i, 0, j], top)
            face_up = weighted_sum(lambda i: last_ref[i, 0, j], bottom)

            @pl.when(place[0] >= 0)
            def _():
                out_ref[place[0], pl.ds(halo_at + j, 1), :] = face_down[:1]

            @pl.when(place[1] >= 0)
            def _():
                out_ref[place[1], pl.ds(halo_at + j, 1), :] = face_up[-1:]

    row_at = pl.multiple_of(step * rows, rows)
    adj = [adj_ref[i, pl.ds(row_at, rows), :] for i in range(variables)]
    span_code = sublane_iota(spans)
    place_code = sublane_iota(SPAN)
    left = []
    right = []
    for corner in range(corners):
        ids = node_ref[corner]
        span = ids >> SPAN_BITS
        owner_rows = NODE_DEV // SPAN
        span = (span & (owner_rows - 1)) * peers + (span >> (owner_rows.bit_length() - 1))
        span = as_code(span)
        inside = as_code(ids & (SPAN - 1))
        values = []
        for x in range(coords):
            values.extend(two_parts(weighted_sum(lambda i: metric_ref[i, x, corner], adj)))
        for r in range(rows):
            hit = span_code == span[r : r + 1]
            left.append(jnp.concatenate([jnp.where(hit, v[r : r + 1], zero) for v in values], axis=0))
            right.append(jnp.where(place_code == inside[r : r + 1], one, zero))
    added = lax.dot_general(
        jnp.concatenate(left, axis=1),
        jnp.concatenate(right, axis=1),
        LAST_WITH_LAST,
        preferred_element_type=jnp.float32,
    )
    totals[...] = jnp.where(step == 0, 0.0, totals[...]) + added

    share = fringe_ref.shape[0]
    row_code = sublane_iota(row_count)
    for q in range(share):
        cell = fringe_ref[pl.ds(q, 1), :]
        column = as_code(cell & (width - 1))
        row = cell >> (width.bit_length() - 1)
        pick = jnp.where(sublane_iota(width) == column, one, zero)
        found = jnp.dot(
            split_adj[...],
            jnp.concatenate([pick, pick], axis=0),
            preferred_element_type=jnp.float32,
        )
        mine = lax.broadcasted_iota(jnp.int32, (row_count, width), 0) == row
        for i in range(variables):
            part = found[i * row_count : (i + 1) * row_count]
            line = jnp.sum(jnp.where(mine, part, 0.0), axis=0, keepdims=True)
            out_ref[step * share + q, pl.ds(payload_at + i, 1), :] = line

    @pl.when(step == steps - 1)
    def _():
        for x in range(coords):
            both = totals[pl.ds(2 * x * spans, spans), :] + totals[pl.ds((2 * x + 1) * spans, spans), :]
            for part in range(NODE_DEV // SPAN):
                for half in range(span_rows):
                    at = (x * (NODE_DEV // SPAN) + part) * span_rows + half
                    out_ref[:, at, :] = both[part * peers : (part + 1) * peers, half * width : (half + 1) * width]


def jacobian(adj_ref, diag_ref, face_ref, out_ref, carry):
    step = pl.program_id(0)
    variables, rows, width = adj_ref.shape
    row_at = pl.multiple_of(step * rows, rows)
    adj = [adj_ref[i] for i in range(variables)]
    row_ids = lax.broadcasted_iota(jnp.int32, (rows, width), 0)
    lane_ids = lax.broadcasted_iota(jnp.int32, (rows, width), 1)

    @pl.when(step == 0)
    def _():
        carry[...] = jnp.zeros_like(carry)

    for j in range(variables):
        total = weighted_sum(lambda i: diag_ref[i, j], adj)
        faces = [weighted_sum(lambda i: face_ref[i, f, j], adj) for f in range(4)]
        below = pltpu.roll(faces[0], rows - 1, 0)
        total = total + jnp.where(row_ids < rows - 1, below, 0.0)
        above = pltpu.roll(faces[1], 1, 0)
        total = total + jnp.where(row_ids > 0, above, carry[pl.ds(j, 1), :])
        right = pltpu.roll(faces[2], width - 1, 1)
        total = total + jnp.where(lane_ids < width - 1, right, 0.0)
        left = pltpu.roll(faces[3], 1, 1)
        total = total + jnp.where(lane_ids > 0, left, 0.0)
        out_ref[j, pl.ds(row_at, rows), :] = total
        carry[pl.ds(j, 1), :] = faces[1][rows - 1 :]

        @pl.when(step > 0)
        def _():
            out_ref[j, pl.ds(row_at - 1, 1), :] += faces[0][:1]


def finish(place, count_ref, recv_ref, cell_ref, weight_ref, base_ref, out_ref, sens_ref):
    variables, row_count, width = base_ref.shape
    peers = recv_ref.shape[0]
    coords = sens_ref.shape[0]
    node_rows = coords * NODE_DEV // width
    payload_at = node_rows
    halo_at = node_rows + variables
    spans = row_count * width // SPAN
    span_rows = SPAN // width
    zero = jnp.zeros((), jnp.bfloat16)
    one = jnp.ones((), jnp.bfloat16)

    sums = jnp.sum(recv_ref[:, :node_rows, :], axis=0)
    per_coord = node_rows // coords
    for x in range(coords):
        for part in range(per_coord):
            at = x * per_coord + part
            sens_ref[pl.ds(x, 1), pl.ds(part * width, width)] = sums[at : at + 1]

    span_code = sublane_iota(spans)
    place_code = sublane_iota(SPAN)
    slot = lax.broadcasted_iota(jnp.int32, (1, width), 1)
    chunk = min(CHUNK, peers)
    for start in range(0, peers, chunk):
        left = []
        right = []
        for q in range(start, start + chunk):
            weight = jnp.where(slot < count_ref[0, q], weight_ref[pl.ds(q, 1), :], 0.0)
            values = two_parts(-(recv_ref[q, pl.ds(payload_at, variables), :] * weight))
            cell = cell_ref[pl.ds(q, 1), :]
            hit = span_code == as_code(cell >> SPAN_BITS)
            left.append(
                jnp.concatenate(
                    [jnp.where(hit, v[i : i + 1], zero) for i in range(variables) for v in values], axis=0
                )
            )
            right.append(jnp.where(place_code == as_code(cell & (SPAN - 1)), one, zero))
        added = lax.dot_general(
            jnp.concatenate(left, axis=1),
            jnp.concatenate(right, axis=1),
            LAST_WITH_LAST,
            preferred_element_type=jnp.float32,
        )
        source = base_ref if start == 0 else out_ref
        for i in range(variables):
            both = added[2 * i * spans : (2 * i + 1) * spans] + added[(2 * i + 1) * spans : (2 * i + 2) * spans]
            for half in range(span_rows):
                where = pl.ds(half, spans, stride=span_rows)
                out_ref[i, where, :] = source[i, where, :] + both[:, half * width : (half + 1) * width]

    @pl.when(place[0] >= 0)
    def _():
        out_ref[:, :1, :] += recv_ref[place[0], pl.ds(halo_at, variables), :].reshape(variables, 1, width)

    @pl.when(place[1] >= 0)
    def _():
        out_ref[:, row_count - 1 :, :] += recv_ref[place[1], pl.ds(halo_at, variables), :].reshape(
            variables, 1, width
        )


def local(
    adjoint,
    jac_diag,
    jac_face,
    metric,
    node_id,
    fringe_cell,
    donor_cell,
    fringe_weight,
    donor_count,
):
    adj, diag, face, met = adjoint[0], jac_diag[0], jac_face[0], metric[0]
    variables, row_count, width = adj.shape
    faces = face.shape[1]
    coords, corners = met.shape[1:3]
    doms, grids = lax.axis_size("dom"), lax.axis_size("grid")
    peers = doms * grids
    node_rows = coords * NODE_DEV // width
    used = node_rows + 2 * variables
    sent_rows = ceil_to(used, 8)
    spans = peers * NODE_DEV // SPAN
    here, lane = lax.axis_index("dom"), lax.axis_index("grid")
    before = jnp.where(here > 0, (here - 1) * grids + lane, -1)
    after = jnp.where(here < doms - 1, (here + 1) * grids + lane, -1)
    place = jnp.stack([before, after]).astype(jnp.int32)
    params = pltpu.CompilerParams(vmem_limit_bytes=VMEM_BYTES)

    rows = 16 if spans <= 64 else 8
    steps = row_count // rows
    share = peers // steps
    edge = 8
    sent = pl.pallas_call(
        gather_and_nodes,
        grid_spec=pltpu.PrefetchScalarGridSpec(
            num_scalar_prefetch=1,
            grid=(steps,),
            in_specs=[
                pl.BlockSpec((variables, row_count, width), lambda s, p: (0, 0, 0)),
                pl.BlockSpec((variables, coords, corners, rows, width), lambda s, p: (0, 0, 0, s, 0)),
                pl.BlockSpec((corners, rows, width), lambda s, p: (0, s, 0)),
                pl.BlockSpec((pl.Squeezed(), share, width), lambda s, p: (s, 0, 0)),
                pl.BlockSpec((variables, 1, variables, edge, width), lambda s, p: (0, 0, 0, 0, 0)),
                pl.BlockSpec(
                    (variables, 1, variables, edge, width), lambda s, p: (0, 1, 0, row_count // edge - 1, 0)
                ),
            ],
            out_specs=pl.BlockSpec((peers, sent_rows, width), lambda s, p: (0, 0, 0)),
            scratch_shapes=[
                pltpu.VMEM((2 * coords * spans, SPAN), jnp.float32),
                pltpu.VMEM((variables * row_count, 2 * width), jnp.bfloat16),
            ],
        ),
        out_shape=jax.ShapeDtypeStruct((peers, sent_rows, width), jnp.float32),
        compiler_params=params,
        cost_estimate=pl.CostEstimate(
            flops=4 * coords * spans * SPAN * corners * row_count * width,
            bytes_accessed=met.size * 4,
            transcendentals=0,
        ),
        name="gather_and_nodes",
    )(place, adj, met, node_id[0], fringe_cell[0].reshape(steps, share, width), face, face)

    received = lax.all_to_all(sent, ("dom", "grid"), split_axis=0, concat_axis=0, tiled=True)

    jac_rows = 16
    base = pl.pallas_call(
        jacobian,
        grid=(row_count // jac_rows,),
        in_specs=[
            pl.BlockSpec((variables, jac_rows, width), lambda s: (0, s, 0)),
            pl.BlockSpec((variables, variables, jac_rows, width), lambda s: (0, 0, s, 0)),
            pl.BlockSpec((variables, faces, variables, jac_rows, width), lambda s: (0, 0, 0, s, 0)),
        ],
        out_specs=pl.BlockSpec((variables, row_count, width), lambda s: (0, 0, 0)),
        out_shape=jax.ShapeDtypeStruct((variables, row_count, width), jnp.float32),
        scratch_shapes=[pltpu.VMEM((8, width), jnp.float32)],
        compiler_params=params,
        cost_estimate=pl.CostEstimate(
            flops=2 * (diag.size + face.size), bytes_accessed=4 * (diag.size + face.size), transcendentals=0
        ),
        name="jacobian",
    )(adj, diag, face)

    vmem = pl.BlockSpec(memory_space=pltpu.VMEM)
    smem = pl.BlockSpec(memory_space=pltpu.SMEM)
    product, node_sens = pl.pallas_call(
        finish,
        in_specs=[smem, smem, vmem, vmem, vmem, vmem],
        out_specs=[vmem, vmem],
        out_shape=[
            jax.ShapeDtypeStruct((variables, row_count, width), jnp.float32),
            jax.ShapeDtypeStruct((coords, NODE_DEV), jnp.float32),
        ],
        compiler_params=params,
        name="finish",
    )(place, donor_count, received, donor_cell[0], fringe_weight[0], base)
    return (product[None], node_sens)


def solution(mesh):
    in_specs = (
        P("grid", None, "dom", None),
        P("grid", None, None, "dom", None),
        P("grid", None, None, None, "dom", None),
        P("grid", None, None, None, "dom", None),
        P("grid", None, "dom", None),
        P(("dom", "grid"), None, None),
        P(("dom", "grid"), None, None),
        P(("dom", "grid"), None, None),
        P(("dom", "grid"), None),
    )
    out_specs = (P("grid", None, "dom", None), P(None, ("dom", "grid")))
    return jax.shard_map(local, mesh=mesh, in_specs=in_specs, out_specs=out_specs, check_vma=False)
```

time: 582 us -> 53.9 us (0.09)
  other arithmetic: 390 us -> 0.08 us
  waiting for transfers between devices: 112 us -> 5.06 us
  local copies, waits for them, and re-layouts: 51.7 us -> 7.55 us
  Pallas kernels: 0 us -> 32.7 us
  between operations: 14.2 us -> 0.69 us
  starting transfers between devices: 13.2 us -> 7.29 us
    scatter-add x2 -> x0, other arithmetic: 378 us -> none  [the longest x1 351 us: local(): partial_value = jnp.zeros((corner_terms.shape[0], node_total), jnp.float3...]
    reduce_scatter x1 -> x0, waiting for transfers between devices: 112 us -> none  [local(): lax.psum_scatter(partial_value, ('dom', 'grid'), scatter_dimension=1, til...]
    pallas_call x0 -> x3, Pallas kernels: none -> 32.7 us  [the longest x1 21.4 us: local(): pl.pallas_call(gather_and_nodes, grid_spec=pltpu.PrefetchScalarGridSpec(n...]
    gather x2 -> x0, local copies, waits for them, and re-layouts: 19.8 us -> none  [local(): payload = jnp.take(flat_values, fringe_cell[0], axis=1)]
    add x1 -> x0, local copies, waits for them, and re-layouts: 16.5 us -> none  [contract(): running = running + blocks[variable] * adjoint_local[variable]]
    add x2 -> x0, other arithmetic: 7.75 us -> none  [contract(): running = running + blocks[variable] * adjoint_local[variable]]
    ppermute x2 -> x0, starting transfers between devices: 6.76 us -> none  [shifted(): return lax.ppermute(block, axis, route)]
  transfers between devices with their start and end apart: 4 -> 1, of which waited for: 1 -> 1; matrix products, arithmetic and copies ran while one was open for 75% -> 0% of each run, Pallas kernels for 0% -> 15%
where the time goes in v1:
time: 53.9 us; the launch traced here: 53.3 us
  Pallas kernels  32.7 us (61%)
  local copies, waits for them, and re-layouts  7.55 us (14%)
  starting transfers between devices  7.29 us (14%)
  waiting for transfers between devices  5.06 us (9%)
  between operations  0.69 us (1%)
    pallas_call x1, Pallas kernels, local(): pl.pallas_call(gather_and_nodes, grid_spec=pltpu.PrefetchScalarGridSpec(n...  21.4 us
    pallas_call x1, Pallas kernels, local(): pl.pallas_call(jacobian, grid=(row_count // jac_rows,), in_specs=[pl.Bloc...  8.09 us
    unnamed x22, local copies, waits for them, and re-layouts  7.55 us
    all_to_all x1, starting transfers between devices, local(): lax.all_to_all(sent, ('dom', 'grid'), split_axis=0, concat_axis=0, tiled=...  7.29 us
    all_to_all x1, waiting for transfers between devices, local(): lax.all_to_all(sent, ('dom', 'grid'), split_axis=0, concat_axis=0, tiled=...  5.06 us
    pallas_call x1, Pallas kernels, local(): pl.pallas_call(finish, in_specs=[smem, smem, vmem, vmem, vmem, vmem], out...  3.13 us
  transfers between devices with their start and end apart: 1, of which 1 were waited for; matrix products, arithmetic and copies ran while one was open for 0% of the time, Pallas kernels for 15%

profile of v1, /device:TPU:0, one launch (start us, length us, event | category | flops | bytes accessed | tf_op | source)
XLA Modules:
  0.0 53.3 jit_solution(14503125447360305022)
XLA Ops:
  0.6 0.1 pad_add_fusion.place
  0.7 0.0 copy-start.6
  0.7 0.5 copy-done.6
  1.2 0.0 copy-start.1
  1.2 1.0 %copy-done.1 = f32[1,6,128,128]{3,2,1,0:T(8,128)S(1)} copy-done((f32[1,6,128,128]{3,2,1,0:T(8,128)S(1)}, f32[1,6,128,128]{3,2,1,0:T(8,128)}, u32[]{:S(2)}) %copy-start.1) | copy-done | bytes 393240
  2.2 0.0 copy-start.8
  2.2 2.3 %copy-done.8 = f32[1,6,3,4,128,128]{5,4,3,2,1,0:T(8,128)S(1)} copy-done((f32[1,6,3,4,128,128]{5,4,3,2,1,0:T(8,128)S(1)}, f32[1,6,3,4,128,128]{5,4,3,2,1,0:T(8,128)}, u32[]{:S(2)}) %copy-start.8) | copy-done | bytes 4718616
  4.6 0.0 copy-start.9
  4.6 0.9 %copy-done.9 = s32[1,4,128,128]{3,2,1,0:T(8,128)S(1)} copy-done((s32[1,4,128,128]{3,2,1,0:T(8,128)S(1)}, s32[1,4,128,128]{3,2,1,0:T(8,128)}, u32[]{:S(2)}) %copy-start.9) | copy-done | bytes 262168
  5.5 0.0 copy-start.10
  5.5 0.7 %copy-done.10 = s32[1,32,128]{2,1,0:T(8,128)S(1)} copy-done((s32[1,32,128]{2,1,0:T(8,128)S(1)}, s32[1,32,128]{2,1,0:T(8,128)}, u32[]{:S(2)}) %copy-start.10) | copy-done | bytes 16408
  6.2 0.0 copy-start
  6.2 0.0 copy-start.2
  6.2 21.4 %gather_and_nodes.1 = f32[32,24,128]{2,1,0:T(8,128)} custom-call(s32[2]{0:T(128)S(1)} %pad_add_fusion.place, f32[6,128,128]{2,1,0:T(8,128)S(1)} %bitcast.12, f32[6,3,4,128,128]{4,3,2,1,0:T(8,128)S(1)} %bitcast.16, s32[4,128,128]{2,1,0:T(8,128)S(1)} %bitcast.17, s32[8,4,128]{2,1,0:T(4,128)S(1)} %bitcast.18, f32[6,4,6,128,128]{4,3,2,1,0:T(8,128)} %bitcast.19, ...), custom_call_target="tpu_custom_call" | custom-call | flops 12884901888 | bytes 4718592 | tf_op jit(solution)/shard_map/gather_and_nodes/pallas_call | solution.py:259
  27.7 7.3 %all-to-all-start = ((f32[32,24,128]{2,1,0:T(8,128)}), f32[32,24,128]{2,1,0:T(8,128)S(1)}, u32[]{:S(2)}, u32[]{:S(2)}) async-start(f32[32,24,128]{2,1,0:T(8,128)} %gather_and_nodes.1), calls=%async_computation | async-start | bytes 786432 | tf_op jit(solution)/shard_map/all_to_all | solution.py:290
  35.0 0.0 copy-done
  35.0 0.0 copy-done.2
  35.0 0.0 copy-start.3
  35.0 8.1 %jacobian.1.base_ref = f32[6,128,128]{2,1,0:T(8,128)S(1)} custom-call(f32[6,128,128]{2,1,0:T(8,128)S(1)} %bitcast.13, f32[6,6,128,128]{3,2,1,0:T(8,128)S(1)} %bitcast.11, f32[6,4,6,128,128]{4,3,2,1,0:T(8,128)} %bitcast.21), custom_call_target="tpu_custom_call" | custom-call | flops 5898240 | bytes 11796480 | tf_op jit(solution)/shard_map/jacobian/pallas_call | solution.py:293
  43.1 5.1 %all-to-all-done.recv_ref = f32[32,24,128]{2,1,0:T(8,128)S(1)} async-done(((f32[32,24,128]{2,1,0:T(8,128)}), f32[32,24,128]{2,1,0:T(8,128)S(1)}, u32[]{:S(2)}, u32[]{:S(2)}) %all-to-all-start) | async-done | bytes 393248 | tf_op jit(solution)/shard_map/all_to_all | solution.py:290
  48.1 0.0 copy-done.3
  48.1 0.0 copy-start.4
  48.2 0.7 %copy-done.4 = f32[1,32,128]{2,1,0:T(8,128)S(1)} copy-done((f32[1,32,128]{2,1,0:T(8,128)S(1)}, f32[1,32,128]{2,1,0:T(8,128)}, u32[]{:S(2)}) %copy-start.4) | copy-done | bytes 16408
  48.9 0.0 copy-start.5
  48.9 0.7 %copy-done.5 = s32[1,32]{1,0:T(1,128)S(1)} copy-done((s32[1,32]{1,0:T(1,128)S(1)}, s32[1,32]{1,0:T(1,128)}, u32[]{:S(2)}) %copy-start.5) | copy-done | bytes 152
  49.5 0.0 copy-start.7
  49.5 0.7 %copy-done.7 = s32[2]{0:T(128)S(1)} copy-done((s32[2]{0:T(128)S(1)}, s32[2]{0:T(128)}, u32[]{:S(2)}) %copy-start.7) | copy-done | bytes 32
  50.2 3.1 %finish.1 = (f32[6,128,128]{2,1,0:T(8,128)}, f32[3,512]{1,0:T(4,128)}) custom-call(s32[2]{0:T(128)S(1)} %copy-done.7, s32[1,32]{1,0:T(1,128)S(1)} %copy-done.5, f32[32,24,128]{2,1,0:T(8,128)S(1)} %all-to-all-done.recv_ref, s32[32,128]{1,0:T(8,128)S(1)} %bitcast.14, f32[32,128]{1,0:T(8,128)S(1)} %bitcast.15, f32[6,128,128]{2,1,0:T(8,128)S(1)} %jacobian.1.base_ref), custom_call_target="tpu_custom_call" | custom-call | tf_op jit(solution)/shard_map/finish/pallas_call | solution.py:313
Async XLA Ops:
  0.7 0.5 copy-start.6
  1.2 1.0 %copy-start.1 = (f32[1,6,128,128]{3,2,1,0:T(8,128)S(1)}, f32[1,6,128,128]{3,2,1,0:T(8,128)}, u32[]{:S(2)}) copy-start(f32[1,6,128,128]{3,2,1,0:T(8,128)} %param.9) | copy-start | bytes 1179652
  2.2 2.3 %copy-start.8 = (f32[1,6,3,4,128,128]{5,4,3,2,1,0:T(8,128)S(1)}, f32[1,6,3,4,128,128]{5,4,3,2,1,0:T(8,128)}, u32[]{:S(2)}) copy-start(f32[1,6,3,4,128,128]{5,4,3,2,1,0:T(8,128)} %param.12) | copy-start | bytes 14155780
  4.6 0.9 %copy-start.9 = (s32[1,4,128,128]{3,2,1,0:T(8,128)S(1)}, s32[1,4,128,128]{3,2,1,0:T(8,128)}, u32[]{:S(2)}) copy-start(s32[1,4,128,128]{3,2,1,0:T(8,128)} %param.13) | copy-start | bytes 786436
  5.5 0.7 %copy-start.10 = (s32[1,32,128]{2,1,0:T(8,128)S(1)}, s32[1,32,128]{2,1,0:T(8,128)}, u32[]{:S(2)}) copy-start(s32[1,32,128]{2,1,0:T(8,128)} %param.14) | copy-start | bytes 49156
  6.2 28.7 %copy-start = (f32[1,6,6,128,128]{4,3,2,1,0:T(8,128)S(1)}, f32[1,6,6,128,128]{4,3,2,1,0:T(8,128)}, u32[]{:S(2)}) copy-start(f32[1,6,6,128,128]{4,3,2,1,0:T(8,128)} %param.10) | copy-start | bytes 7077892
  6.2 28.7 %copy-start.2 = (f32[1,6,128,128]{3,2,1,0:T(8,128)S(1)}, f32[1,6,128,128]{3,2,1,0:T(8,128)}, u32[]{:S(2)}) copy-start(f32[1,6,128,128]{3,2,1,0:T(8,128)} %param.9) | copy-start | bytes 1179652
  27.7 20.5 %all-to-all-start = ((f32[32,24,128]{2,1,0:T(8,128)}), f32[32,24,128]{2,1,0:T(8,128)S(1)}, u32[]{:S(2)}, u32[]{:S(2)}) async-start(f32[32,24,128]{2,1,0:T(8,128)} %gather_and_nodes.1), calls=%async_computation | async-start | bytes 786432 | tf_op jit(solution)/shard_map/all_to_all | solution.py:290
  35.0 13.2 %copy-start.3 = (s32[1,32,128]{2,1,0:T(8,128)S(1)}, s32[1,32,128]{2,1,0:T(8,128)}, u32[]{:S(2)}) copy-start(s32[1,32,128]{2,1,0:T(8,128)} %param.15) | copy-start | bytes 49156
  48.1 0.7 %copy-start.4 = (f32[1,32,128]{2,1,0:T(8,128)S(1)}, f32[1,32,128]{2,1,0:T(8,128)}, u32[]{:S(2)}) copy-start(f32[1,32,128]{2,1,0:T(8,128)} %param.16) | copy-start | bytes 49156
  48.9 0.7 %copy-start.5 = (s32[1,32]{1,0:T(1,128)S(1)}, s32[1,32]{1,0:T(1,128)}, u32[]{:S(2)}) copy-start(s32[1,32]{1,0:T(1,128)} %count_ref.1) | copy-start | bytes 388
  49.5 0.7 %copy-start.7 = (s32[2]{0:T(128)S(1)}, s32[2]{0:T(128)}, u32[]{:S(2)}) copy-start(s32[2]{0:T(128)} %copy-done.6) | copy-start | bytes 28

commit v2 on v1

--- a/solution.py
+++ b/solution.py
@@ -12,7 +12,7 @@
 SPAN = 256
 SPAN_BITS = SPAN.bit_length() - 1
 CHUNK = 32
-VMEM_BYTES = 48 * 1024 * 1024
+VMEM_BYTES = 62 * 1024 * 1024
 LAST_WITH_LAST = (((1,), (1,)), ((), ()))
 
 

time: 53.9 us -> 48.1 us (0.89)
  local copies, waits for them, and re-layouts: 7.55 us -> 0.75 us
  Pallas kernels: 32.7 us -> 34.4 us
  waiting for transfers between devices: 5.06 us -> 3.99 us
    unnamed x22 -> x2, local copies, waits for them, and re-layouts: 7.55 us -> 0.75 us
    pallas_call x1, Pallas kernels: 8.09 us -> 9.18 us  [local(): pl.pallas_call(jacobian, grid=(row_count // jac_rows,), in_specs=[pl.Bloc...]
    all_to_all x1, waiting for transfers between devices: 5.06 us -> 3.99 us  [local(): lax.all_to_all(sent, ('dom', 'grid'), split_axis=0, concat_axis=0, tiled=...]
    pallas_call x1, Pallas kernels: 3.13 us -> 3.75 us  [local(): pl.pallas_call(finish, in_specs=[smem, smem, vmem, vmem, vmem, vmem], out...]
  transfers between devices with their start and end apart: 1 -> 1, of which waited for: 1 -> 1; matrix products, arithmetic and copies ran while one was open for 0% -> 0% of each run, Pallas kernels for 15% -> 19%
where the time goes in v2:
time: 48.1 us; the launch traced here: 47.7 us
  Pallas kernels  34.4 us (72%)
  starting transfers between devices  7.29 us (15%)
  waiting for transfers between devices  3.99 us (8%)
  local copies, waits for them, and re-layouts  0.75 us (2%)
  between operations  0.66 us (1%)
  other arithmetic  0.61 us (1%)
    pallas_call x1, Pallas kernels, local(): pl.pallas_call(gather_and_nodes, grid_spec=pltpu.PrefetchScalarGridSpec(n...  21.4 us
    pallas_call x1, Pallas kernels, local(): pl.pallas_call(jacobian, grid=(row_count // jac_rows,), in_specs=[pl.Bloc...  9.18 us
    all_to_all x1, starting transfers between devices, local(): lax.all_to_all(sent, ('dom', 'grid'), split_axis=0, concat_axis=0, tiled=...  7.29 us
    all_to_all x1, waiting for transfers between devices, local(): lax.all_to_all(sent, ('dom', 'grid'), split_axis=0, concat_axis=0, tiled=...  3.99 us
    pallas_call x1, Pallas kernels, local(): pl.pallas_call(finish, in_specs=[smem, smem, vmem, vmem, vmem, vmem], out...  3.75 us
  transfers between devices with their start and end apart: 1, of which 1 were waited for; matrix products, arithmetic and copies ran while one was open for 0% of the time, Pallas kernels for 19%

profile of v2, /device:TPU:0, one launch (start us, length us, event | category | flops | bytes accessed | tf_op | source)
XLA Modules:
  0.0 47.7 jit_solution(5226928558600296342)
XLA Ops:
  0.6 0.6 %pad_add_fusion.place = s32[2]{0:T(128)} fusion(s32[1]{0:T(128)} %bitcast.1, s32[1]{0:T(128)} %bitcast), kind=kLoop, calls=%fused_computation | loop fusion | flops 2 | bytes 16 | tf_op jit(solution)/shard_map/stack | solution.py:252
  1.3 21.4 %gather_and_nodes.1 = f32[32,24,128]{2,1,0:T(8,128)} custom-call(s32[2]{0:T(128)} %pad_add_fusion.place, f32[6,128,128]{2,1,0:T(8,128)} %bitcast.15, f32[6,3,4,128,128]{4,3,2,1,0:T(8,128)} %bitcast.19, s32[4,128,128]{2,1,0:T(8,128)} %bitcast.21, s32[8,4,128]{2,1,0:T(4,128)} %bitcast.22, f32[6,4,6,128,128]{4,3,2,1,0:T(8,128)} %bitcast.11, ...), custom_call_target="tpu_custom_call" | custom-call | flops 12884901888 | bytes 4718592 | tf_op jit(solution)/shard_map/gather_and_nodes/pallas_call | solution.py:259
  22.7 7.3 %all-to-all-start = ((f32[32,24,128]{2,1,0:T(8,128)}), f32[32,24,128]{2,1,0:T(8,128)S(1)}, u32[]{:S(2)}, u32[]{:S(2)}) async-start(f32[32,24,128]{2,1,0:T(8,128)} %gather_and_nodes.1), calls=%async_computation | async-start | bytes 786432 | tf_op jit(solution)/shard_map/all_to_all | solution.py:290
  30.0 9.2 %jacobian.1.base_ref = f32[6,128,128]{2,1,0:T(8,128)} custom-call(f32[6,128,128]{2,1,0:T(8,128)} %bitcast.16, f32[6,6,128,128]{3,2,1,0:T(8,128)} %bitcast.14, f32[6,4,6,128,128]{4,3,2,1,0:T(8,128)} %bitcast.13), custom_call_target="tpu_custom_call" | custom-call | flops 5898240 | bytes 11796480 | tf_op jit(solution)/shard_map/jacobian/pallas_call | solution.py:293
  39.2 4.0 %all-to-all-done.recv_ref = f32[32,24,128]{2,1,0:T(8,128)S(1)} async-done(((f32[32,24,128]{2,1,0:T(8,128)}), f32[32,24,128]{2,1,0:T(8,128)S(1)}, u32[]{:S(2)}, u32[]{:S(2)}) %all-to-all-start) | async-done | bytes 393248 | tf_op jit(solution)/shard_map/all_to_all | solution.py:290
  43.2 0.0 copy-start
  43.2 0.8 %copy-done = f32[32,24,128]{2,1,0:T(8,128)} copy-done((f32[32,24,128]{2,1,0:T(8,128)}, f32[32,24,128]{2,1,0:T(8,128)S(1)}, u32[]{:S(2)}) %copy-start) | copy-done | bytes 393240
  43.9 3.7 %finish.1 = (f32[6,128,128]{2,1,0:T(8,128)}, f32[3,512]{1,0:T(4,128)}) custom-call(s32[2]{0:T(128)} %pad_add_fusion.place, s32[1,32]{1,0:T(1,128)} %count_ref.1, f32[32,24,128]{2,1,0:T(8,128)} %copy-done, s32[32,128]{1,0:T(8,128)} %bitcast.17, f32[32,128]{1,0:T(8,128)} %bitcast.18, f32[6,128,128]{2,1,0:T(8,128)} %jacobian.1.base_ref), custom_call_target="tpu_custom_call" | custom-call | tf_op jit(solution)/shard_map/finish/pallas_call | solution.py:313
Async XLA Ops:
  22.7 20.5 %all-to-all-start = ((f32[32,24,128]{2,1,0:T(8,128)}), f32[32,24,128]{2,1,0:T(8,128)S(1)}, u32[]{:S(2)}, u32[]{:S(2)}) async-start(f32[32,24,128]{2,1,0:T(8,128)} %gather_and_nodes.1), calls=%async_computation | async-start | bytes 786432 | tf_op jit(solution)/shard_map/all_to_all | solution.py:290
  43.2 0.8 %copy-start = (f32[32,24,128]{2,1,0:T(8,128)}, f32[32,24,128]{2,1,0:T(8,128)S(1)}, u32[]{:S(2)}) copy-start(f32[32,24,128]{2,1,0:T(8,128)S(1)} %all-to-all-done.recv_ref) | copy-start | bytes 1179652

commit v3 on v2

v3 whole, which is shorter than its diff:
```python
import functools

import jax
import jax.numpy as jnp
from jax import lax
from jax.experimental import pallas as pl
from jax.experimental.pallas import tpu as pltpu
from jax.sharding import PartitionSpec as P

NODE_DEV = 512
LANES = 128
SPAN = 256
SPAN_BITS = SPAN.bit_length() - 1
CHUNK = 32
VMEM_BYTES = 62 * 1024 * 1024
LAST_WITH_LAST = (((1,), (1,)), ((), ()))


def neighbours(dom="dom", grid="grid"):
    here, lane = lax.axis_index(dom), lax.axis_index(grid)
    doms, grids = lax.axis_size(dom), lax.axis_size(grid)
    before, after = (here - 1) * grids + lane, (here + 1) * grids + lane
    return here > 0, before, here < doms - 1, after


def ceil_to(value, unit):
    return -(-value // unit) * unit


def sublane_iota(count):
    return lax.broadcasted_iota(jnp.int32, (count, LANES), 0).astype(jnp.bfloat16)


def as_code(index):
    return index.astype(jnp.float32).astype(jnp.bfloat16)


def two_parts(value):
    head = value.astype(jnp.bfloat16)
    tail = (value - head.astype(jnp.float32)).astype(jnp.bfloat16)
    return head, tail


def weighted_sum(load, adj):
    running = load(0) * adj[0]
    for variable in range(1, len(adj)):
        running = running + load(variable) * adj[variable]
    return running


def gather_and_nodes(
    adj_ref, metric_ref, node_ref, fringe_ref, first_ref, last_ref, out_ref, totals, split_adj
):
    step = pl.program_id(0)
    steps = pl.num_programs(0)
    variables, row_count, width = adj_ref.shape
    coords, corners, rows = metric_ref.shape[1:4]
    peers = out_ref.shape[0]
    spans = totals.shape[0] // (2 * coords)
    span_rows = SPAN // width
    node_rows = coords * NODE_DEV // width
    payload_at = node_rows
    halo_at = node_rows + variables
    zero = jnp.zeros((), jnp.bfloat16)
    one = jnp.ones((), jnp.bfloat16)

    @pl.when(step == 0)
    def _():
        head, tail = two_parts(adj_ref[...].reshape(variables * row_count, width))
        split_adj[:, :width] = head
        split_adj[:, width:] = tail
        out_ref[:, halo_at:, :] = jnp.zeros((peers, out_ref.shape[1] - halo_at, width), jnp.float32)
        top = [adj_ref[i, : first_ref.shape[3], :] for i in range(variables)]
        bottom = [adj_ref[i, row_count - last_ref.shape[3] :, :] for i in range(variables)]
        has_before, before, has_after, after = neighbours()
        for j in range(variables):
            face_down = weighted_sum(lambda i: first_ref[i, 0, j], top)
            face_up = weighted_sum(lambda i: last_ref[i, 0, j], bottom)

            @pl.when(has_before)
            def _():
                out_ref[before, pl.ds(halo_at + j, 1), :] = face_down[:1]

            @pl.when(has_after)
            def _():
                out_ref[after, pl.ds(halo_at + j, 1), :] = face_up[-1:]

    row_at = pl.multiple_of(step * rows, rows)
    adj = [adj_ref[i, pl.ds(row_at, rows), :] for i in range(variables)]
    span_code = sublane_iota(spans)
    place_code = sublane_iota(SPAN)
    left = []
    right = []
    for corner in range(corners):
        ids = node_ref[corner]
        span = ids >> SPAN_BITS
        owner_rows = NODE_DEV // SPAN
        span = (span & (owner_rows - 1)) * peers + (span >> (owner_rows.bit_length() - 1))
        span = as_code(span)
        inside = as_code(ids & (SPAN - 1))
        values = []
        for x in range(coords):
            values.extend(two_parts(weighted_sum(lambda i: metric_ref[i, x, corner], adj)))
        for r in range(rows):
            hit = span_code == span[r : r + 1]
            left.append(jnp.concatenate([jnp.where(hit, v[r : r + 1], zero) for v in values], axis=0))
            right.append(jnp.where(place_code == inside[r : r + 1], one, zero))
    added = lax.dot_general(
        jnp.concatenate(left, axis=1),
        jnp.concatenate(right, axis=1),
        LAST_WITH_LAST,
        preferred_element_type=jnp.float32,
    )
    totals[...] = jnp.where(step == 0, 0.0, totals[...]) + added

    share = fringe_ref.shape[0]
    column_code = sublane_iota(width)
    row_ids = lax.broadcasted_iota(jnp.int32, (row_count, width), 0)
    picks = []
    for q in range(share):
        pick = jnp.where(column_code == as_code(fringe_ref[pl.ds(q, 1), :] & (width - 1)), one, zero)
        picks.append(jnp.concatenate([pick, pick], axis=0))
    found = jnp.dot(split_adj[...], jnp.concatenate(picks, axis=1), preferred_element_type=jnp.float32)
    for q in range(share):
        mine = row_ids == fringe_ref[pl.ds(q, 1), :] >> (width.bit_length() - 1)
        for i in range(variables):
            part = found[i * row_count : (i + 1) * row_count, q * width : (q + 1) * width]
            line = jnp.sum(jnp.where(mine, part, 0.0), axis=0, keepdims=True)
            out_ref[step * share + q, pl.ds(payload_at + i, 1), :] = line

    @pl.when(step == steps - 1)
    def _():
        for x in range(coords):
            both = totals[pl.ds(2 * x * spans, spans), :] + totals[pl.ds((2 * x + 1) * spans, spans), :]
            for part in range(NODE_DEV // SPAN):
                for half in range(span_rows):
                    at = (x * (NODE_DEV // SPAN) + part) * span_rows + half
                    out_ref[:, at, :] = both[part * peers : (part + 1) * peers, half * width : (half + 1) * width]


def jacobian(count_ref, weight_ref, adj_ref, diag_ref, face_ref, out_ref, minus_ref):
    variables, row_count, width = adj_ref.shape
    peers = weight_ref.shape[0]

    @pl.when(pl.program_id(0) == 0)
    def _():
        slot = lax.broadcasted_iota(jnp.int32, (1, width), 1)
        for q in range(peers):
            minus_ref[pl.ds(q, 1), :] = jnp.where(slot < count_ref[0, q], -weight_ref[pl.ds(q, 1), :], 0.0)

    adj = [adj_ref[i] for i in range(variables)]
    row_ids = lax.broadcasted_iota(jnp.int32, (row_count, width), 0)
    lane_ids = lax.broadcasted_iota(jnp.int32, (row_count, width), 1)
    total = weighted_sum(lambda i: diag_ref[i], adj)
    faces = [weighted_sum(lambda i: face_ref[i, f], adj) for f in range(4)]
    below = pltpu.roll(faces[0], row_count - 1, 0)
    total = total + jnp.where(row_ids < row_count - 1, below, 0.0)
    above = pltpu.roll(faces[1], 1, 0)
    total = total + jnp.where(row_ids > 0, above, 0.0)
    right = pltpu.roll(faces[2], width - 1, 1)
    total = total + jnp.where(lane_ids < width - 1, right, 0.0)
    left = pltpu.roll(faces[3], 1, 1)
    out_ref[...] = total + jnp.where(lane_ids > 0, left, 0.0)


def finish(recv_ref, cell_ref, weight_ref, base_ref, out_ref, sens_ref):
    variables, row_count, width = base_ref.shape
    peers = recv_ref.shape[0]
    coords = sens_ref.shape[0]
    node_rows = coords * NODE_DEV // width
    payload_at = node_rows
    halo_at = node_rows + variables
    spans = row_count * width // SPAN
    span_rows = SPAN // width
    zero = jnp.zeros((), jnp.bfloat16)
    one = jnp.ones((), jnp.bfloat16)

    sums = jnp.sum(recv_ref[:, :node_rows, :], axis=0)
    per_coord = node_rows // coords
    for x in range(coords):
        for part in range(per_coord):
            at = x * per_coord + part
            sens_ref[pl.ds(x, 1), pl.ds(part * width, width)] = sums[at : at + 1]

    span_code = sublane_iota(spans)
    place_code = sublane_iota(SPAN)
    chunk = min(CHUNK, peers)
    for start in range(0, peers, chunk):
        left = []
        right = []
        for q in range(start, start + chunk):
            weight = weight_ref[pl.ds(q, 1), :]
            values = two_parts(recv_ref[q, pl.ds(payload_at, variables), :] * weight)
            cell = cell_ref[pl.ds(q, 1), :]
            hit = span_code == as_code(cell >> SPAN_BITS)
            left.append(
                jnp.concatenate(
                    [jnp.where(hit, v[i : i + 1], zero) for i in range(variables) for v in values], axis=0
                )
            )
            right.append(jnp.where(place_code == as_code(cell & (SPAN - 1)), one, zero))
        added = lax.dot_general(
            jnp.concatenate(left, axis=1),
            jnp.concatenate(right, axis=1),
            LAST_WITH_LAST,
            preferred_element_type=jnp.float32,
        )
        source = base_ref if start == 0 else out_ref
        for i in range(variables):
            both = added[2 * i * spans : (2 * i + 1) * spans] + added[(2 * i + 1) * spans : (2 * i + 2) * spans]
            for half in range(span_rows):
                where = pl.ds(half, spans, stride=span_rows)
                out_ref[i, where, :] = source[i, where, :] + both[:, half * width : (half + 1) * width]

    has_before, before, has_after, after = neighbours()

    @pl.when(has_before)
    def _():
        out_ref[:, :1, :] += recv_ref[before, pl.ds(halo_at, variables), :].reshape(variables, 1, width)

    @pl.when(has_after)
    def _():
        out_ref[:, row_count - 1 :, :] += recv_ref[after, pl.ds(halo_at, variables), :].reshape(
            variables, 1, width
        )


def local(
    adjoint,
    jac_diag,
    jac_face,
    metric,
    node_id,
    fringe_cell,
    donor_cell,
    fringe_weight,
    donor_count,
):
    adj, diag, face, met = adjoint[0], jac_diag[0], jac_face[0], metric[0]
    variables, row_count, width = adj.shape
    faces = face.shape[1]
    coords, corners = met.shape[1:3]
    doms, grids = lax.axis_size("dom"), lax.axis_size("grid")
    peers = doms * grids
    node_rows = coords * NODE_DEV // width
    used = node_rows + 2 * variables
    sent_rows = ceil_to(used, 8)
    spans = peers * NODE_DEV // SPAN
    params = pltpu.CompilerParams(vmem_limit_bytes=VMEM_BYTES)

    rows = 16 if spans <= 64 else 8
    steps = row_count // rows
    share = peers // steps
    edge = 8
    sent = pl.pallas_call(
        gather_and_nodes,
        grid=(steps,),
        in_specs=[
            pl.BlockSpec((variables, row_count, width), lambda s: (0, 0, 0)),
            pl.BlockSpec((variables, coords, corners, rows, width), lambda s: (0, 0, 0, s, 0)),
            pl.BlockSpec((corners, rows, width), lambda s: (0, s, 0)),
            pl.BlockSpec((pl.Squeezed(), share, width), lambda s: (s, 0, 0)),
            pl.BlockSpec((variables, 1, variables, edge, width), lambda s: (0, 0, 0, 0, 0)),
            pl.BlockSpec((variables, 1, variables, edge, width), lambda s: (0, 1, 0, row_count // edge - 1, 0)),
        ],
        out_specs=pl.BlockSpec((peers, sent_rows, width), lambda s: (0, 0, 0)),
        scratch_shapes=[
            pltpu.VMEM((2 * coords * spans, SPAN), jnp.float32),
            pltpu.VMEM((variables * row_count, 2 * width), jnp.bfloat16),
        ],
        out_shape=jax.ShapeDtypeStruct((peers, sent_rows, width), jnp.float32),
        compiler_params=pltpu.CompilerParams(vmem_limit_bytes=62 * 1024 * 1024),
        cost_estimate=pl.CostEstimate(
            flops=4 * coords * spans * SPAN * corners * row_count * width,
            bytes_accessed=met.size * 4,
            transcendentals=0,
        ),
        name="gather_and_nodes",
    )(adj, met, node_id[0], fringe_cell[0].reshape(steps, share, width), face, face)

    received = lax.all_to_all(sent, ("dom", "grid"), split_axis=0, concat_axis=0, tiled=True)

    vmem = pl.BlockSpec(memory_space=pltpu.VMEM)
    base, minus_weight = pl.pallas_call(
        jacobian,
        grid=(variables,),
        in_specs=[
            pl.BlockSpec(memory_space=pltpu.SMEM),
            pl.BlockSpec((peers, width), lambda j: (0, 0)),
            pl.BlockSpec((variables, row_count, width), lambda j: (0, 0, 0)),
            pl.BlockSpec((variables, pl.Squeezed(), row_count, width), lambda j: (0, j, 0, 0)),
            pl.BlockSpec((variables, faces, pl.Squeezed(), row_count, width), lambda j: (0, 0, j, 0, 0)),
        ],
        out_specs=[
            pl.BlockSpec((pl.Squeezed(), row_count, width), lambda j: (j, 0, 0)),
            pl.BlockSpec((peers, width), lambda j: (0, 0)),
        ],
        out_shape=[
            jax.ShapeDtypeStruct((variables, row_count, width), jnp.float32),
            jax.ShapeDtypeStruct((peers, width), jnp.float32),
        ],
        compiler_params=pltpu.CompilerParams(vmem_limit_bytes=40 * 1024 * 1024),
        cost_estimate=pl.CostEstimate(
            flops=2 * (diag.size + face.size), bytes_accessed=4 * (diag.size + face.size), transcendentals=0
        ),
        name="jacobian",
    )(donor_count, fringe_weight[0], adj, diag, face)

    product, node_sens = pl.pallas_call(
        finish,
        in_specs=[vmem] * 4,
        out_specs=[vmem] * 2,
        out_shape=[
            jax.ShapeDtypeStruct((variables, row_count, width), jnp.float32),
            jax.ShapeDtypeStruct((coords, NODE_DEV), jnp.float32),
        ],
        compiler_params=pltpu.CompilerParams(vmem_limit_bytes=20 * 1024 * 1024),
        name="finish",
    )(received, donor_cell[0], minus_weight, base)
    return (product[None], node_sens)


def solution(mesh):
    in_specs = (
        P("grid", None, "dom", None),
        P("grid", None, None, "dom", None),
        P("grid", None, None, None, "dom", None),
        P("grid", None, None, None, "dom", None),
        P("grid", None, "dom", None),
        P(("dom", "grid"), None, None),
        P(("dom", "grid"), None, None),
        P(("dom", "grid"), None, None),
        P(("dom", "grid"), None),
    )
    out_specs = (P("grid", None, "dom", None), P(None, ("dom", "grid")))
    return jax.shard_map(local, mesh=mesh, in_specs=in_specs, out_specs=out_specs, check_vma=False)
```

time: 48.1 us -> 43.1 us (0.90)
  Pallas kernels: 34.4 us -> 24.2 us
  local copies, waits for them, and re-layouts: 0.75 us -> 5.36 us
  waiting for transfers between devices: 3.99 us -> 5.32 us
  other arithmetic: 0.61 us -> 0 us
    pallas_call x3, Pallas kernels: 34.4 us -> 24.2 us  [the longest x1 19.1 us: local(): pl.pallas_call(gather_and_nodes, grid=(steps,), in_specs=[pl.BlockSpec((v...]
    unnamed x2 -> x12, local copies, waits for them, and re-layouts: 0.75 us -> 5.36 us
    all_to_all x1, waiting for transfers between devices: 3.99 us -> 5.32 us  [local(): lax.all_to_all(sent, ('dom', 'grid'), split_axis=0, concat_axis=0, tiled=...]
    another operation x1 -> x0, other arithmetic: 0.61 us -> none  [local(): place = jnp.stack([before, after]).astype(jnp.int32)]
  transfers between devices with their start and end apart: 1 -> 1, of which waited for: 1 -> 1; matrix products, arithmetic and copies ran while one was open for 0% -> 0% of each run, Pallas kernels for 19% -> 6%
where the time goes in v3:
time: 43.1 us; the launch traced here: 42.9 us
  Pallas kernels  24.2 us (56%)
  starting transfers between devices  7.3 us (17%)
  local copies, waits for them, and re-layouts  5.36 us (12%)
  waiting for transfers between devices  5.32 us (12%)
  between operations  0.71 us (2%)
    pallas_call x1, Pallas kernels, local(): pl.pallas_call(gather_and_nodes, grid=(steps,), in_specs=[pl.BlockSpec((v...  19.1 us
    all_to_all x1, starting transfers between devices, local(): lax.all_to_all(sent, ('dom', 'grid'), split_axis=0, concat_axis=0, tiled=...  7.3 us
    unnamed x12, local copies, waits for them, and re-layouts  5.36 us
    all_to_all x1, waiting for transfers between devices, local(): lax.all_to_all(sent, ('dom', 'grid'), split_axis=0, concat_axis=0, tiled=...  5.32 us
    pallas_call x1, Pallas kernels, local(): pl.pallas_call(finish, in_specs=[vmem] * 4, out_specs=[vmem] * 2, out_sha...  2.59 us
    pallas_call x1, Pallas kernels, local(): pl.pallas_call(jacobian, grid=(variables,), in_specs=[pl.BlockSpec(memory...  2.47 us
  transfers between devices with their start and end apart: 1, of which 1 were waited for; matrix products, arithmetic and copies ran while one was open for 0% of the time, Pallas kernels for 6%

profile of v3, /device:TPU:0, one launch (start us, length us, event | category | flops | bytes accessed | tf_op | source)
XLA Modules:
  0.0 42.9 jit_solution(10762015077303464716)
XLA Ops:
  0.6 0.0 copy-start.2
  0.6 0.0 copy-start.3
  0.7 0.0 copy-start.5
  0.7 19.1 %gather_and_nodes.1 = f32[32,24,128]{2,1,0:T(8,128)} custom-call(f32[6,128,128]{2,1,0:T(8,128)} %bitcast.13, f32[6,3,4,128,128]{4,3,2,1,0:T(8,128)} %bitcast.17, s32[4,128,128]{2,1,0:T(8,128)} %bitcast.19, s32[8,4,128]{2,1,0:T(4,128)} %bitcast.20, f32[6,4,6,128,128]{4,3,2,1,0:T(8,128)} %bitcast.9, f32[6,4,6,128,128]{4,3,2,1,0:T(8,128)} %bitcast.10), custom_call_target="tpu_custom_call" | custom-call | flops 12884901888 | bytes 4718592 | tf_op jit(solution)/shard_map/gather_and_nodes/pallas_call | solution.py:255
  19.8 7.3 %all-to-all-start = ((f32[32,24,128]{2,1,0:T(8,128)}), f32[32,24,128]{2,1,0:T(8,128)S(1)}, u32[]{:S(2)}, u32[]{:S(2)}) async-start(f32[32,24,128]{2,1,0:T(8,128)} %gather_and_nodes.1), calls=%async_computation | async-start | bytes 786432 | tf_op jit(solution)/shard_map/all_to_all | solution.py:281
  27.1 0.0 copy-done.2
  27.1 0.0 copy-done.3
  27.1 0.0 copy-done.5
  27.1 0.0 copy-start
  27.1 3.7 %copy-done = f32[1,6,4,6,128,128]{5,4,3,2,1,0:T(8,128)S(1)} copy-done((f32[1,6,4,6,128,128]{5,4,3,2,1,0:T(8,128)S(1)}, f32[1,6,4,6,128,128]{5,4,3,2,1,0:T(8,128)}, u32[]{:S(2)}) %copy-start) | copy-done | bytes 9437208
  30.8 0.0 copy-start.1
  30.8 1.7 %copy-done.1 = f32[1,6,6,128,128]{4,3,2,1,0:T(8,128)S(1)} copy-done((f32[1,6,6,128,128]{4,3,2,1,0:T(8,128)S(1)}, f32[1,6,6,128,128]{4,3,2,1,0:T(8,128)}, u32[]{:S(2)}) %copy-start.1) | copy-done | bytes 2359320
  32.5 0.0 copy-start.4
  32.5 2.5 %jacobian.1 = (f32[6,128,128]{2,1,0:T(8,128)S(1)}, f32[32,128]{1,0:T(8,128)S(1)}) custom-call(s32[1,32]{1,0:T(1,128)S(1)} %copy-done.5, f32[32,128]{1,0:T(8,128)S(1)} %bitcast.15, f32[6,128,128]{2,1,0:T(8,128)S(1)} %bitcast.14, f32[6,6,128,128]{3,2,1,0:T(8,128)S(1)} %bitcast.12, f32[6,4,6,128,128]{4,3,2,1,0:T(8,128)S(1)} %bitcast.11), custom_call_target="tpu_custom_call" | custom-call | flops 5898240 | bytes 11796480 | tf_op jit(solution)/shard_map/jacobian/pallas_call | solution.py:284
  34.9 5.3 %all-to-all-done.recv_ref = f32[32,24,128]{2,1,0:T(8,128)S(1)} async-done(((f32[32,24,128]{2,1,0:T(8,128)}), f32[32,24,128]{2,1,0:T(8,128)S(1)}, u32[]{:S(2)}, u32[]{:S(2)}) %all-to-all-start) | async-done | bytes 393248 | tf_op jit(solution)/shard_map/all_to_all | solution.py:281
  40.3 0.0 copy-done.4
  40.3 2.6 %finish.1 = (f32[6,128,128]{2,1,0:T(8,128)}, f32[3,512]{1,0:T(4,128)}) custom-call(f32[32,24,128]{2,1,0:T(8,128)S(1)} %all-to-all-done.recv_ref, s32[32,128]{1,0:T(8,128)S(1)} %bitcast.16, f32[32,128]{1,0:T(8,128)S(1)} %get-tuple-element.6.weight_ref, f32[6,128,128]{2,1,0:T(8,128)S(1)} %get-tuple-element.7.base_ref), custom_call_target="tpu_custom_call" | custom-call | tf_op jit(solution)/shard_map/finish/pallas_call | solution.py:309
Async XLA Ops:
  0.6 26.5 %copy-start.2 = (f32[1,6,128,128]{3,2,1,0:T(8,128)S(1)}, f32[1,6,128,128]{3,2,1,0:T(8,128)}, u32[]{:S(2)}) copy-start(f32[1,6,128,128]{3,2,1,0:T(8,128)} %param.9) | copy-start | bytes 1179652
  0.6 26.5 %copy-start.3 = (f32[1,32,128]{2,1,0:T(8,128)S(1)}, f32[1,32,128]{2,1,0:T(8,128)}, u32[]{:S(2)}) copy-start(f32[1,32,128]{2,1,0:T(8,128)} %param.16) | copy-start | bytes 49156
  0.7 26.5 %copy-start.5 = (s32[1,32]{1,0:T(1,128)S(1)}, s32[1,32]{1,0:T(1,128)}, u32[]{:S(2)}) copy-start(s32[1,32]{1,0:T(1,128)} %count_ref.1) | copy-start | bytes 388
  19.8 20.5 %all-to-all-start = ((f32[32,24,128]{2,1,0:T(8,128)}), f32[32,24,128]{2,1,0:T(8,128)S(1)}, u32[]{:S(2)}, u32[]{:S(2)}) async-start(f32[32,24,128]{2,1,0:T(8,128)} %gather_and_nodes.1), calls=%async_computation | async-start | bytes 786432 | tf_op jit(solution)/shard_map/all_to_all | solution.py:281
  27.1 3.7 %copy-start = (f32[1,6,4,6,128,128]{5,4,3,2,1,0:T(8,128)S(1)}, f32[1,6,4,6,128,128]{5,4,3,2,1,0:T(8,128)}, u32[]{:S(2)}) copy-start(f32[1,6,4,6,128,128]{5,4,3,2,1,0:T(8,128)} %param.11) | copy-start | bytes 28311556
  30.8 1.7 %copy-start.1 = (f32[1,6,6,128,128]{4,3,2,1,0:T(8,128)S(1)}, f32[1,6,6,128,128]{4,3,2,1,0:T(8,128)}, u32[]{:S(2)}) copy-start(f32[1,6,6,128,128]{4,3,2,1,0:T(8,128)} %param.10) | copy-start | bytes 7077892
  32.5 7.8 %copy-start.4 = (s32[1,32,128]{2,1,0:T(8,128)S(1)}, s32[1,32,128]{2,1,0:T(8,128)}, u32[]{:S(2)}) copy-start(s32[1,32,128]{2,1,0:T(8,128)} %param.15) | copy-start | bytes 49156

commit v4 on v0

v4 whole, which is shorter than its diff:
```python
import functools

import jax
import jax.numpy as jnp
from jax import lax
from jax.experimental import pallas as pl
from jax.experimental.pallas import tpu as pltpu
from jax.sharding import PartitionSpec as P

NODE_DEV = 512
LANES = 128
SPAN = 256
SPAN_BITS = SPAN.bit_length() - 1
CHUNK = 32
GROUP = 16
PAIR = 2
ROWS = 32
VMEM_BYTES = 62 * 1024 * 1024
LAST_WITH_LAST = (((1,), (1,)), ((), ()))


def shifted(block, axis, distance):
    devices = range(lax.axis_size(axis))
    route = [(i - distance, i) for i in devices if i - distance in devices]
    return lax.ppermute(block, axis, route)


def sublane_iota(count):
    return lax.broadcasted_iota(jnp.int32, (count, LANES), 0).astype(jnp.bfloat16)


def as_code(index):
    return index.astype(jnp.float32).astype(jnp.bfloat16)


def two_parts(value):
    head = value.astype(jnp.bfloat16)
    tail = (value - head.astype(jnp.float32)).astype(jnp.bfloat16)
    return head, tail


def weighted_sum(load, adj):
    running = load(0) * adj[0]
    for variable in range(1, len(adj)):
        running = running + load(variable) * adj[variable]
    return running


def cells_and_nodes(
    adj_ref,
    fringe_ref,
    node_ref,
    metric_hbm,
    diag_hbm,
    face_hbm,
    sent_ref,
    down_ref,
    up_ref,
    base_ref,
    totals,
    split_adj,
    metric_part,
    diag_part,
    face_part,
    edge_down,
    edge_up,
    metric_sem,
    diag_sem,
    face_sem,
):
    variables, row_count, width = adj_ref.shape
    steps, _, coords, corners, rows = metric_part.shape[:5]
    peers = sent_ref.shape[0]
    spans = totals.shape[0] // (2 * coords)
    span_rows = SPAN // width
    cell_spans = row_count // span_rows
    payload_at = coords * NODE_DEV // width
    zero = jnp.zeros((), jnp.bfloat16)
    one = jnp.ones((), jnp.bfloat16)

    def copies(step):
        at = pl.ds(pl.multiple_of(step * rows, rows), rows)
        return (
            pltpu.make_async_copy(metric_hbm.at[:, :, :, at, :], metric_part.at[step], metric_sem.at[step]),
            pltpu.make_async_copy(diag_hbm.at[:, :, at, :], diag_part.at[step], diag_sem.at[step]),
            pltpu.make_async_copy(face_hbm.at[:, :, :, at, :], face_part.at[step], face_sem.at[step]),
        )

    for step in range(steps):
        for copy in copies(step):
            copy.start()

    for i in range(variables):
        for half in range(span_rows):
            for part, piece in enumerate(two_parts(adj_ref[i, pl.ds(half, cell_spans, stride=span_rows), :])):
                at = part * SPAN + half * width
                split_adj[pl.ds(i * cell_spans, cell_spans), pl.ds(at, width)] = piece
    totals[...] = jnp.zeros_like(totals)

    place_code = sublane_iota(SPAN)
    cell_rows = lax.broadcasted_iota(jnp.int32, (cell_spans, width), 0)
    group = min(GROUP, peers)

    def gather(turn, none):
        picks = []
        for k in range(group):
            inside = fringe_ref[pl.ds(turn * group + k, 1), :] & (SPAN - 1)
            pick = jnp.where(place_code == as_code(inside), one, zero)
            picks.append(jnp.concatenate([pick, pick], axis=0))
        found = jnp.dot(split_adj[...], jnp.concatenate(picks, axis=1), preferred_element_type=jnp.float32)
        for k in range(group):
            q = turn * group + k
            mine = cell_rows == fringe_ref[pl.ds(q, 1), :] >> SPAN_BITS
            for i in range(variables):
                part = found[i * cell_spans : (i + 1) * cell_spans, k * width : (k + 1) * width]
                line = jnp.sum(jnp.where(mine, part, 0.0), axis=0, keepdims=True)
                at = payload_at + i
                sent_ref[q, at // PAIR, pl.ds(at % PAIR, 1), :] = line
        return none

    lax.fori_loop(0, peers // group, gather, 0)

    span_code = sublane_iota(spans)
    row_ids = lax.broadcasted_iota(jnp.int32, (rows, width), 0)
    lane_ids = lax.broadcasted_iota(jnp.int32, (rows, width), 1)

    def cells(step, none):
        for copy in copies(step):
            copy.wait()
        here = pl.ds(pl.multiple_of(step * rows, rows), rows)
        adj = [adj_ref[i, here, :] for i in range(variables)]
        for j in range(variables):
            total = weighted_sum(lambda i: diag_part[step, i, j], adj)
            faces = [weighted_sum(lambda i: face_part[step, i, f, j], adj) for f in range(4)]
            below = pltpu.roll(faces[0], rows - 1, 0)
            total = total + jnp.where(row_ids < rows - 1, below, 0.0)
            above = pltpu.roll(faces[1], 1, 0)
            total = total + jnp.where(row_ids > 0, above, 0.0)
            right = pltpu.roll(faces[2], width - 1, 1)
            total = total + jnp.where(lane_ids < width - 1, right, 0.0)
            left = pltpu.roll(faces[3], 1, 1)
            base_ref[j, here, :] = total + jnp.where(lane_ids > 0, left, 0.0)
            edge_down[step, pl.ds(j, 1), :] = faces[0][:1]
            edge_up[step, pl.ds(j, 1), :] = faces[1][rows - 1 :]

        left = []
        right = []
        for corner in range(corners):
            ids = node_ref[corner, here, :]
            span = ids >> SPAN_BITS
            owner_rows = NODE_DEV // SPAN
            span = (span & (owner_rows - 1)) * peers + (span >> (owner_rows.bit_length() - 1))
            span = as_code(span)
            inside = as_code(ids & (SPAN - 1))
            values = []
            for x in range(coords):
                values.extend(two_parts(weighted_sum(lambda i: metric_part[step, i, x, corner], adj)))
            for r in range(rows):
                hit = span_code == span[r : r + 1]
                left.append(jnp.concatenate([jnp.where(hit, v[r : r + 1], zero) for v in values], axis=0))
                right.append(jnp.where(place_code == inside[r : r + 1], one, zero))
        added = lax.dot_general(
            jnp.concatenate(left, axis=1),
            jnp.concatenate(right, axis=1),
            LAST_WITH_LAST,
            preferred_element_type=jnp.float32,
        )
        totals[...] = totals[...] + added
        return none

    lax.fori_loop(0, steps, cells, 0)

    for step in range(1, steps):
        for j in range(variables):
            base_ref[j, pl.ds(step * rows - 1, 1), :] += edge_down[step, pl.ds(j, 1), :]
            base_ref[j, pl.ds(step * rows, 1), :] += edge_up[step - 1, pl.ds(j, 1), :]
    down_ref[...] = edge_down[0, :variables, :]
    up_ref[...] = edge_up[steps - 1, :variables, :]

    for x in range(coords):
        both = totals[pl.ds(2 * x * spans, spans), :] + totals[pl.ds((2 * x + 1) * spans, spans), :]
        for part in range(NODE_DEV // SPAN):
            for half in range(span_rows):
                at = (x * (NODE_DEV // SPAN) + part) * span_rows + half
                sent_ref[:, at // PAIR, at % PAIR, :] = both[
                    part * peers : (part + 1) * peers, half * width : (half + 1) * width
                ]


def prepare(count_ref, weight_ref, base_ref, minus_ref, out_ref):
    peers, width = weight_ref.shape
    slot = lax.broadcasted_iota(jnp.int32, (1, width), 1)
    for q in range(peers):
        minus_ref[pl.ds(q, 1), :] = jnp.where(slot < count_ref[0, q], -weight_ref[pl.ds(q, 1), :], 0.0)
    out_ref[...] = base_ref[...]


def finish(recv_ref, down_ref, up_ref, cell_ref, weight_ref, base_ref, out_ref, sens_ref):
    variables, row_count, width = base_ref.shape
    peers = recv_ref.shape[0]
    coords = sens_ref.shape[0]
    node_rows = coords * NODE_DEV // width
    payload_at = node_rows
    spans = row_count * width // SPAN
    span_rows = SPAN // width
    zero = jnp.zeros((), jnp.bfloat16)
    one = jnp.ones((), jnp.bfloat16)

    sums = [jnp.sum(recv_ref[:, at, :, :], axis=0) for at in range(node_rows // PAIR)]
    per_coord = node_rows // coords
    for x in range(coords):
        for part in range(per_coord):
            at = x * per_coord + part
            sens_ref[pl.ds(x, 1), pl.ds(part * width, width)] = sums[at // PAIR][at % PAIR : at % PAIR + 1]

    span_code = sublane_iota(spans)
    place_code = sublane_iota(SPAN)
    payload = []
    for i in range(variables):
        at = payload_at + i
        payload.append(two_parts(recv_ref[:, at // PAIR, at % PAIR, :] * weight_ref[...]))
    chunk = min(CHUNK, peers)
    for start in range(0, peers, chunk):
        left = []
        right = []
        for q in range(start, start + chunk):
            cell = cell_ref[pl.ds(q, 1), :]
            hit = span_code == as_code(cell >> SPAN_BITS)
            left.append(
                jnp.concatenate(
                    [jnp.where(hit, v[q : q + 1], zero) for values in payload for v in values], axis=0
                )
            )
            right.append(jnp.where(place_code == as_code(cell & (SPAN - 1)), one, zero))
        added = lax.dot_general(
            jnp.concatenate(left, axis=1),
            jnp.concatenate(right, axis=1),
            LAST_WITH_LAST,
            preferred_element_type=jnp.float32,
        )
        source = base_ref if start == 0 else out_ref
        for i in range(variables):
            both = added[2 * i * spans : (2 * i + 1) * spans] + added[(2 * i + 1) * spans : (2 * i + 2) * spans]
            for half in range(span_rows):
                where = pl.ds(half, spans, stride=span_rows)
                out_ref[i, where, :] = source[i, where, :] + both[:, half * width : (half + 1) * width]

    for i in range(variables):
        out_ref[i, pl.ds(row_count - 1, 1), :] += down_ref[pl.ds(i, 1), :]
        out_ref[i, pl.ds(0, 1), :] += up_ref[pl.ds(i, 1), :]


def local(
    adjoint,
    jac_diag,
    jac_face,
    metric,
    node_id,
    fringe_cell,
    donor_cell,
    fringe_weight,
    donor_count,
):
    adj, diag, face, met = adjoint[0], jac_diag[0], jac_face[0], metric[0]
    variables, row_count, width = adj.shape
    faces = face.shape[1]
    coords, corners = met.shape[1:3]
    doms, grids = lax.axis_size("dom"), lax.axis_size("grid")
    peers = doms * grids
    node_rows = coords * NODE_DEV // width
    sent_shape = (peers, (node_rows + variables) // PAIR, PAIR, width)
    spans = peers * NODE_DEV // SPAN
    params = pltpu.CompilerParams(vmem_limit_bytes=VMEM_BYTES)

    rows = ROWS if spans <= 64 else 8
    steps = row_count // rows
    vmem = pl.BlockSpec(memory_space=pltpu.VMEM)
    smem = pl.BlockSpec(memory_space=pltpu.SMEM)
    hbm = pl.BlockSpec(memory_space=pl.ANY)
    sent, down, up, base = pl.pallas_call(
        cells_and_nodes,
        in_specs=[vmem] * 3 + [hbm] * 3,
        out_specs=[vmem] * 4,
        out_shape=[
            jax.ShapeDtypeStruct(sent_shape, jnp.float32),
            jax.ShapeDtypeStruct((variables, width), jnp.float32),
            jax.ShapeDtypeStruct((variables, width), jnp.float32),
            jax.ShapeDtypeStruct((variables, row_count, width), jnp.float32),
        ],
        scratch_shapes=[
            pltpu.VMEM((2 * coords * spans, SPAN), jnp.float32),
            pltpu.VMEM((variables * row_count * width // SPAN, 2 * SPAN), jnp.bfloat16),
            pltpu.VMEM((steps, variables, coords, corners, rows, width), jnp.float32),
            pltpu.VMEM((steps, variables, variables, rows, width), jnp.float32),
            pltpu.VMEM((steps, variables, faces, variables, rows, width), jnp.float32),
            pltpu.VMEM((steps, 8, width), jnp.float32),
            pltpu.VMEM((steps, 8, width), jnp.float32),
            pltpu.SemaphoreType.DMA((steps,)),
            pltpu.SemaphoreType.DMA((steps,)),
            pltpu.SemaphoreType.DMA((steps,)),
        ],
        compiler_params=pltpu.CompilerParams(vmem_limit_bytes=VMEM_BYTES),
        cost_estimate=pl.CostEstimate(
            flops=4 * coords * spans * SPAN * corners * row_count * width,
            bytes_accessed=4 * (met.size + diag.size + face.size),
            transcendentals=0,
        ),
        name="cells_and_nodes",
    )(adj, fringe_cell[0], node_id[0], met, diag, face)

    received = lax.all_to_all(sent, ("dom", "grid"), split_axis=0, concat_axis=0, tiled=True)
    from_below = shifted(down, "dom", -1)
    from_above = shifted(up, "dom", 1)

    minus_weight, held = pl.pallas_call(
        prepare,
        in_specs=[smem] + [vmem] * 2,
        out_specs=[vmem] * 2,
        out_shape=[
            jax.ShapeDtypeStruct((peers, width), jnp.float32),
            jax.ShapeDtypeStruct((variables, row_count, width), jnp.float32),
        ],
        compiler_params=pltpu.CompilerParams(vmem_limit_bytes=20 * 1024 * 1024),
        cost_estimate=pl.CostEstimate(flops=base.size, bytes_accessed=8 * base.size, transcendentals=0),
        name="prepare",
    )(donor_count, fringe_weight[0], base)

    product, node_sens = pl.pallas_call(
        finish,
        in_specs=[vmem] * 6,
        out_specs=[vmem] * 2,
        out_shape=[
            jax.ShapeDtypeStruct((variables, row_count, width), jnp.float32),
            jax.ShapeDtypeStruct((coords, NODE_DEV), jnp.float32),
        ],
        compiler_params=pltpu.CompilerParams(vmem_limit_bytes=20 * 1024 * 1024),
        name="finish",
    )(received, from_below, from_above, donor_cell[0], minus_weight, held)
    return (product[None], node_sens)


def solution(mesh):
    in_specs = (
        P("grid", None, "dom", None),
        P("grid", None, None, "dom", None),
        P("grid", None, None, None, "dom", None),
        P("grid", None, None, None, "dom", None),
        P("grid", None, "dom", None),
        P(("dom", "grid"), None, None),
        P(("dom", "grid"), None, None),
        P(("dom", "grid"), None, None),
        P(("dom", "grid"), None),
    )
    out_specs = (P("grid", None, "dom", None), P(None, ("dom", "grid")))
    return jax.shard_map(local, mesh=mesh, in_specs=in_specs, out_specs=out_specs, check_vma=False)
```

time: 582 us -> 40.6 us (0.07)
  other arithmetic: 390 us -> 0 us
  waiting for transfers between devices: 112 us -> 3.92 us
  local copies, waits for them, and re-layouts: 51.7 us -> 1 us
  Pallas kernels: 0 us -> 21.5 us
  between operations: 14.2 us -> 0.74 us
    scatter-add x2 -> x0, other arithmetic: 378 us -> none  [the longest x1 351 us: local(): partial_value = jnp.zeros((corner_terms.shape[0], node_total), jnp.float3...]
    reduce_scatter x1 -> x0, waiting for transfers between devices: 112 us -> none  [local(): lax.psum_scatter(partial_value, ('dom', 'grid'), scatter_dimension=1, til...]
    pallas_call x0 -> x3, Pallas kernels: none -> 21.5 us  [the longest x1 18.4 us: local(): pl.pallas_call(cells_and_nodes, in_specs=[vmem] * 3 + [hbm] * 3, out_spec...]
    gather x2 -> x0, local copies, waits for them, and re-layouts: 19.8 us -> none  [local(): payload = jnp.take(flat_values, fringe_cell[0], axis=1)]
    add x1 -> x0, local copies, waits for them, and re-layouts: 16.5 us -> none  [contract(): running = running + blocks[variable] * adjoint_local[variable]]
    add x2 -> x0, other arithmetic: 7.75 us -> none  [contract(): running = running + blocks[variable] * adjoint_local[variable]]
    unnamed x16 -> x8, local copies, waits for them, and re-layouts: 6.87 us -> 1 us
  transfers between devices with their start and end apart: 4 -> 3, of which waited for: 1 -> 1; matrix products, arithmetic and copies ran while one was open for 75% -> 0% of each run, Pallas kernels for 0% -> 1%
where the time goes in v4:
time: 40.6 us; the launch traced here: 40.3 us
  Pallas kernels  21.5 us (53%)
  starting transfers between devices  13.1 us (32%)
  waiting for transfers between devices  3.92 us (10%)
  local copies, waits for them, and re-layouts  1 us (2%)
  between operations  0.74 us (2%)
    pallas_call x1, Pallas kernels, local(): pl.pallas_call(cells_and_nodes, in_specs=[vmem] * 3 + [hbm] * 3, out_spec...  18.4 us
    all_to_all x1, starting transfers between devices, local(): lax.all_to_all(sent, ('dom', 'grid'), split_axis=0, concat_axis=0, tiled=...  7.3 us
    ppermute x2, starting transfers between devices, shifted(): return lax.ppermute(block, axis, route)  5.84 us
    all_to_all x1, waiting for transfers between devices, local(): lax.all_to_all(sent, ('dom', 'grid'), split_axis=0, concat_axis=0, tiled=...  3.91 us
    pallas_call x1, Pallas kernels, local(): pl.pallas_call(finish, in_specs=[vmem] * 6, out_specs=[vmem] * 2, out_sha...  2.59 us
    unnamed x8, local copies, waits for them, and re-layouts  1 us
  transfers between devices with their start and end apart: 3, of which 1 were waited for; matrix products, arithmetic and copies ran while one was open for 0% of the time, Pallas kernels for 1%

profile of v4, /device:TPU:0, one launch (start us, length us, event | category | flops | bytes accessed | tf_op | source)
XLA Modules:
  0.0 40.3 jit_solution(5345769989868081825)
XLA Ops:
  0.6 0.0 copy-start.1
  0.6 0.0 copy-start.3
  0.7 0.0 copy-start.2
  0.7 18.4 %cells_and_nodes.1 = (f32[32,9,2,128]{3,2,1,0:T(2,128)}, f32[6,128]{1,0:T(8,128)}, f32[6,128]{1,0:T(8,128)}, f32[6,128,128]{2,1,0:T(8,128)}) custom-call(f32[6,128,128]{2,1,0:T(8,128)} %bitcast.14, s32[32,128]{1,0:T(8,128)} %bitcast.17, s32[4,128,128]{2,1,0:T(8,128)} %bitcast.16, f32[6,3,4,128,128]{4,3,2,1,0:T(8,128)} %bitcast.12, ...), custom_call_target="tpu_custom_call" | custom-call | flops 12884901888 | bytes 16515072 | tf_op jit(solution)/shard_map/cells_and_nodes/pallas_call | solution.py:280
  19.0 7.3 %all-to-all-start = ((f32[32,9,2,128]{3,2,1,0:T(2,128)}), f32[32,9,2,128]{3,2,1,0:T(2,128)S(1)}, u32[]{:S(2)}, u32[]{:S(2)}) async-start(f32[32,9,2,128]{3,2,1,0:T(2,128)} %get-tuple-element.10), calls=%async_computation | async-start | bytes 589824 | tf_op jit(solution)/shard_map/all_to_all | solution.py:311
  26.4 1.3 %collective-permute-start = (f32[6,128]{1,0:T(8,128)}, f32[6,128]{1,0:T(8,128)S(1)}, u32[]{:S(2)}, u32[]{:S(2)}) collective-permute-start(f32[6,128]{1,0:T(8,128)} %get-tuple-element.11), channel_id=1, source_target_pairs={{4,0},{8,4},{12,8},{16,12},{20,16},{24,20},{28,24},{5,1},{9,5},{13... | collective-permute-start | bytes 9224 | tf_op jit(solution)/shard_map/ppermute | solution.py:25
  27.7 4.5 %collective-permute-start.1 = (f32[6,128]{1,0:T(8,128)}, f32[6,128]{1,0:T(8,128)S(1)}, u32[]{:S(2)}, u32[]{:S(2)}) collective-permute-start(f32[6,128]{1,0:T(8,128)} %get-tuple-element.12), channel_id=1, source_target_pairs={{0,4},{4,8},{8,12},{12,16},{16,20},{20,24},{24,28},{1,5},{5,9},{9,... | collective-permute-start | bytes 9224 | tf_op jit(solution)/shard_map/ppermute | solution.py:25
  32.2 0.0 copy-done.1
  32.2 0.0 copy-done.3
  32.2 0.0 copy-start
  32.2 1.0 %copy-done = f32[6,128,128]{2,1,0:T(8,128)S(1)} copy-done((f32[6,128,128]{2,1,0:T(8,128)S(1)}, f32[6,128,128]{2,1,0:T(8,128)}, u32[]{:S(2)}) %copy-start) | copy-done | bytes 393240
  33.2 0.6 %prepare.1 = (f32[32,128]{1,0:T(8,128)S(1)}, f32[6,128,128]{2,1,0:T(8,128)S(1)}) custom-call(s32[1,32]{1,0:T(1,128)S(1)} %copy-done.3, f32[32,128]{1,0:T(8,128)S(1)} %bitcast.9, f32[6,128,128]{2,1,0:T(8,128)S(1)} %copy-done), custom_call_target="tpu_custom_call" | custom-call | flops 98304 | bytes 786432 | tf_op jit(solution)/shard_map/prepare/pallas_call | solution.py:315
  33.8 0.0 collective-permute-done.down_ref
  33.8 0.0 collective-permute-done.1.up_ref
  33.8 3.9 %all-to-all-done.recv_ref = f32[32,9,2,128]{3,2,1,0:T(2,128)S(1)} async-done(((f32[32,9,2,128]{3,2,1,0:T(2,128)}), f32[32,9,2,128]{3,2,1,0:T(2,128)S(1)}, u32[]{:S(2)}, u32[]{:S(2)}) %all-to-all-start) | async-done | bytes 294944 | tf_op jit(solution)/shard_map/all_to_all | solution.py:311
  37.8 0.0 copy-done.2
  37.8 2.6 %finish.1 = (f32[6,128,128]{2,1,0:T(8,128)}, f32[3,512]{1,0:T(4,128)}) custom-call(f32[32,9,2,128]{3,2,1,0:T(2,128)S(1)} %all-to-all-done.recv_ref, f32[6,128]{1,0:T(8,128)S(1)} %collective-permute-done.down_ref, f32[6,128]{1,0:T(8,128)S(1)} %collective-permute-done.1.up_ref, s32[32,128]{1,0:T(8,128)S(1)} %bitcast.10, ...), custom_call_target="tpu_custom_call" | custom-call | tf_op jit(solution)/shard_map/finish/pallas_call | solution.py:328
Async XLA Ops:
  0.6 31.6 %copy-start.1 = (f32[1,32,128]{2,1,0:T(8,128)S(1)}, f32[1,32,128]{2,1,0:T(8,128)}, u32[]{:S(2)}) copy-start(f32[1,32,128]{2,1,0:T(8,128)} %param.16) | copy-start | bytes 49156
  0.6 31.6 %copy-start.3 = (s32[1,32]{1,0:T(1,128)S(1)}, s32[1,32]{1,0:T(1,128)}, u32[]{:S(2)}) copy-start(s32[1,32]{1,0:T(1,128)} %count_ref.1) | copy-start | bytes 388
  0.7 37.1 %copy-start.2 = (s32[1,32,128]{2,1,0:T(8,128)S(1)}, s32[1,32,128]{2,1,0:T(8,128)}, u32[]{:S(2)}) copy-start(s32[1,32,128]{2,1,0:T(8,128)} %param.15) | copy-start | bytes 49156
  19.0 18.7 %all-to-all-start = ((f32[32,9,2,128]{3,2,1,0:T(2,128)}), f32[32,9,2,128]{3,2,1,0:T(2,128)S(1)}, u32[]{:S(2)}, u32[]{:S(2)}) async-start(f32[32,9,2,128]{3,2,1,0:T(2,128)} %get-tuple-element.10), calls=%async_computation | async-start | bytes 589824 | tf_op jit(solution)/shard_map/all_to_all | solution.py:311
  26.4 7.5 %collective-permute-start = (f32[6,128]{1,0:T(8,128)}, f32[6,128]{1,0:T(8,128)S(1)}, u32[]{:S(2)}, u32[]{:S(2)}) collective-permute-start(f32[6,128]{1,0:T(8,128)} %get-tuple-element.11), channel_id=1, source_target_pairs={{4,0},{8,4},{12,8},{16,12},{20,16},{24,20},{28,24},{5,1},{9,5},{13... | collective-permute-start | bytes 9224 | tf_op jit(solution)/shard_map/ppermute | solution.py:25
  27.7 6.2 %collective-permute-start.1 = (f32[6,128]{1,0:T(8,128)}, f32[6,128]{1,0:T(8,128)S(1)}, u32[]{:S(2)}, u32[]{:S(2)}) collective-permute-start(f32[6,128]{1,0:T(8,128)} %get-tuple-element.12), channel_id=1, source_target_pairs={{0,4},{4,8},{8,12},{12,16},{16,20},{20,24},{24,28},{1,5},{5,9},{9,... | collective-permute-start | bytes 9224 | tf_op jit(solution)/shard_map/ppermute | solution.py:25
  32.2 1.0 %copy-start = (f32[6,128,128]{2,1,0:T(8,128)S(1)}, f32[6,128,128]{2,1,0:T(8,128)}, u32[]{:S(2)}) copy-start(f32[6,128,128]{2,1,0:T(8,128)} %get-tuple-element.13.base_ref) | copy-start | bytes 1179652

commit v5 on v4

--- a/solution.py
+++ b/solution.py
@@ -12,7 +12,7 @@
 SPAN = 256
 SPAN_BITS = SPAN.bit_length() - 1
 CHUNK = 32
-GROUP = 16
+GROUP = 32
 PAIR = 2
 ROWS = 32
 VMEM_BYTES = 62 * 1024 * 1024
@@ -57,13 +57,13 @@
     down_ref,
     up_ref,
     base_ref,
+    edge_down,
+    edge_up,
     totals,
     split_adj,
     metric_part,
     diag_part,
     face_part,
-    edge_down,
-    edge_up,
     metric_sem,
     diag_sem,
     face_sem,
@@ -170,10 +170,6 @@
 
     lax.fori_loop(0, steps, cells, 0)
 
-    for step in range(1, steps):
-        for j in range(variables):
-            base_ref[j, pl.ds(step * rows - 1, 1), :] += edge_down[step, pl.ds(j, 1), :]
-            base_ref[j, pl.ds(step * rows, 1), :] += edge_up[step - 1, pl.ds(j, 1), :]
     down_ref[...] = edge_down[0, :variables, :]
     up_ref[...] = edge_up[steps - 1, :variables, :]
 
@@ -187,12 +183,19 @@
                 ]
 
 
-def prepare(count_ref, weight_ref, base_ref, minus_ref, out_ref):
+def prepare(count_ref, weight_ref, base_ref, edge_down, edge_up, minus_ref, out_ref):
+    variables, row_count = base_ref.shape[:2]
+    steps = edge_down.shape[0]
+    rows = row_count // steps
     peers, width = weight_ref.shape
     slot = lax.broadcasted_iota(jnp.int32, (1, width), 1)
     for q in range(peers):
         minus_ref[pl.ds(q, 1), :] = jnp.where(slot < count_ref[0, q], -weight_ref[pl.ds(q, 1), :], 0.0)
     out_ref[...] = base_ref[...]
+    for step in range(1, steps):
+        for j in range(variables):
+            out_ref[j, pl.ds(step * rows - 1, 1), :] += edge_down[step, pl.ds(j, 1), :]
+            out_ref[j, pl.ds(step * rows, 1), :] += edge_up[step - 1, pl.ds(j, 1), :]
 
 
 def finish(recv_ref, down_ref, up_ref, cell_ref, weight_ref, base_ref, out_ref, sens_ref):
@@ -277,15 +280,17 @@
     vmem = pl.BlockSpec(memory_space=pltpu.VMEM)
     smem = pl.BlockSpec(memory_space=pltpu.SMEM)
     hbm = pl.BlockSpec(memory_space=pl.ANY)
-    sent, down, up, base = pl.pallas_call(
+    sent, down, up, base, edge_down, edge_up = pl.pallas_call(
         cells_and_nodes,
         in_specs=[vmem] * 3 + [hbm] * 3,
-        out_specs=[vmem] * 4,
+        out_specs=[vmem] * 6,
         out_shape=[
             jax.ShapeDtypeStruct(sent_shape, jnp.float32),
             jax.ShapeDtypeStruct((variables, width), jnp.float32),
             jax.ShapeDtypeStruct((variables, width), jnp.float32),
             jax.ShapeDtypeStruct((variables, row_count, width), jnp.float32),
+            jax.ShapeDtypeStruct((steps, 8, width), jnp.float32),
+            jax.ShapeDtypeStruct((steps, 8, width), jnp.float32),
         ],
         scratch_shapes=[
             pltpu.VMEM((2 * coords * spans, SPAN), jnp.float32),
@@ -293,8 +298,6 @@
             pltpu.VMEM((steps, variables, coords, corners, rows, width), jnp.float32),
             pltpu.VMEM((steps, variables, variables, rows, width), jnp.float32),
             pltpu.VMEM((steps, variables, faces, variables, rows, width), jnp.float32),
-            pltpu.VMEM((steps, 8, width), jnp.float32),
-            pltpu.VMEM((steps, 8, width), jnp.float32),
             pltpu.SemaphoreType.DMA((steps,)),
             pltpu.SemaphoreType.DMA((steps,)),
             pltpu.SemaphoreType.DMA((steps,)),
@@ -314,7 +317,7 @@
 
     minus_weight, held = pl.pallas_call(
         prepare,
-        in_specs=[smem] + [vmem] * 2,
+        in_specs=[smem] + [vmem] * 4,
         out_specs=[vmem] * 2,
         out_shape=[
             jax.ShapeDtypeStruct((peers, width), jnp.float32),
@@ -323,7 +326,7 @@
         compiler_params=pltpu.CompilerParams(vmem_limit_bytes=20 * 1024 * 1024),
         cost_estimate=pl.CostEstimate(flops=base.size, bytes_accessed=8 * base.size, transcendentals=0),
         name="prepare",
-    )(donor_count, fringe_weight[0], base)
+    )(donor_count, fringe_weight[0], base, edge_down, edge_up)
 
     product, node_sens = pl.pallas_call(
         finish,

time: 40.6 us -> 40.9 us (level)
  waiting for transfers between devices: 3.92 us -> 2.46 us
  local copies, waits for them, and re-layouts: 1 us -> 2.44 us
    all_to_all x1, waiting for transfers between devices: 3.91 us -> 2.46 us  [local(): lax.all_to_all(sent, ('dom', 'grid'), split_axis=0, concat_axis=0, tiled=...]
    unnamed x8 -> x12, local copies, waits for them, and re-layouts: 1 us -> 2.44 us
where the time goes in v5:
time: 40.9 us; the launch traced here: 40.5 us
  Pallas kernels  21.7 us (53%)
  starting transfers between devices  13.1 us (32%)
  waiting for transfers between devices  2.46 us (6%)
  local copies, waits for them, and re-layouts  2.44 us (6%)
  between operations  0.74 us (2%)
    pallas_call x1, Pallas kernels, local(): pl.pallas_call(cells_and_nodes, in_specs=[vmem] * 3 + [hbm] * 3, out_spec...  18.5 us
    all_to_all x1, starting transfers between devices, local(): lax.all_to_all(sent, ('dom', 'grid'), split_axis=0, concat_axis=0, tiled=...  7.3 us
    ppermute x2, starting transfers between devices, shifted(): return lax.ppermute(block, axis, route)  5.84 us
    pallas_call x1, Pallas kernels, local(): pl.pallas_call(finish, in_specs=[vmem] * 6, out_specs=[vmem] * 2, out_sha...  2.6 us
    all_to_all x1, waiting for transfers between devices, local(): lax.all_to_all(sent, ('dom', 'grid'), split_axis=0, concat_axis=0, tiled=...  2.46 us
    unnamed x12, local copies, waits for them, and re-layouts  2.44 us
  transfers between devices with their start and end apart: 3, of which 1 were waited for; matrix products, arithmetic and copies ran while one was open for 0% of the time, Pallas kernels for 1%

profile of v5, /device:TPU:0, one launch (start us, length us, event | category | flops | bytes accessed | tf_op | source)
XLA Modules:
  0.0 40.5 jit_solution(14498923035156414938)
XLA Ops:
  0.6 0.0 copy-start.1
  0.6 0.0 copy-start.5
  0.7 0.0 copy-start.2
  0.7 18.5 %cells_and_nodes.1 = (f32[32,9,2,128]{3,2,1,0:T(2,128)}, f32[6,128]{1,0:T(8,128)}, f32[6,128]{1,0:T(8,128)}, f32[6,128,128]{2,1,0:T(8,128)}, f32[4,8,128]{2,1,0:T(8,128)}, /*index=5*/f32[4,8,128]{2,1,0:T(8,128)}) custom-call(f32[6,128,128]{2,1,0:T(8,128)} %bitcast.14, s32[32,128]{1,0:T(8,128)} %bitcast.17, s32[4,128,128]{2,1,0:T(8,128)} %bitcast.16, ...), custom_call_target="tpu_custom_call" | custom-call | flops 12884901888 | bytes 16515072 | tf_op jit(solution)/shard_map/cells_and_nodes/pallas_call | solution.py:283
  19.2 7.3 %all-to-all-start = ((f32[32,9,2,128]{3,2,1,0:T(2,128)}), f32[32,9,2,128]{3,2,1,0:T(2,128)S(1)}, u32[]{:S(2)}, u32[]{:S(2)}) async-start(f32[32,9,2,128]{3,2,1,0:T(2,128)} %get-tuple-element.12), calls=%async_computation | async-start | bytes 589824 | tf_op jit(solution)/shard_map/all_to_all | solution.py:314
  26.5 1.3 %collective-permute-start = (f32[6,128]{1,0:T(8,128)}, f32[6,128]{1,0:T(8,128)S(1)}, u32[]{:S(2)}, u32[]{:S(2)}) collective-permute-start(f32[6,128]{1,0:T(8,128)} %get-tuple-element.13), channel_id=1, source_target_pairs={{4,0},{8,4},{12,8},{16,12},{20,16},{24,20},{28,24},{5,1},{9,5},{13... | collective-permute-start | bytes 9224 | tf_op jit(solution)/shard_map/ppermute | solution.py:25
  27.8 4.5 %collective-permute-start.1 = (f32[6,128]{1,0:T(8,128)}, f32[6,128]{1,0:T(8,128)S(1)}, u32[]{:S(2)}, u32[]{:S(2)}) collective-permute-start(f32[6,128]{1,0:T(8,128)} %get-tuple-element.14), channel_id=1, source_target_pairs={{0,4},{4,8},{8,12},{12,16},{16,20},{20,24},{24,28},{1,5},{5,9},{9,... | collective-permute-start | bytes 9224 | tf_op jit(solution)/shard_map/ppermute | solution.py:25
  32.3 0.0 copy-done.1
  32.3 0.0 copy-done.5
  32.4 0.0 copy-start
  32.4 1.0 %copy-done = f32[6,128,128]{2,1,0:T(8,128)S(1)} copy-done((f32[6,128,128]{2,1,0:T(8,128)S(1)}, f32[6,128,128]{2,1,0:T(8,128)}, u32[]{:S(2)}) %copy-start) | copy-done | bytes 393240
  33.4 0.0 copy-start.3
  33.4 0.7 %copy-done.3 = f32[4,8,128]{2,1,0:T(8,128)S(1)} copy-done((f32[4,8,128]{2,1,0:T(8,128)S(1)}, f32[4,8,128]{2,1,0:T(8,128)}, u32[]{:S(2)}) %copy-start.3) | copy-done | bytes 16408
  34.1 0.0 copy-start.4
  34.1 0.7 %copy-done.4 = f32[4,8,128]{2,1,0:T(8,128)S(1)} copy-done((f32[4,8,128]{2,1,0:T(8,128)S(1)}, f32[4,8,128]{2,1,0:T(8,128)}, u32[]{:S(2)}) %copy-start.4) | copy-done | bytes 16408
  34.8 0.6 %prepare.1 = (f32[32,128]{1,0:T(8,128)S(1)}, f32[6,128,128]{2,1,0:T(8,128)S(1)}) custom-call(s32[1,32]{1,0:T(1,128)S(1)} %copy-done.5, f32[32,128]{1,0:T(8,128)S(1)} %bitcast.9, f32[6,128,128]{2,1,0:T(8,128)S(1)} %copy-done, f32[4,8,128]{2,1,0:T(8,128)S(1)} %copy-done.3, f32[4,8,128]{2,1,0:T(8,128)S(1)} %copy-done.4), custom_call_target="tpu_custom_call" | custom-call | flops 98304 | bytes 786432 | tf_op jit(solution)/shard_map/prepare/pallas_call | solution.py:318
  35.4 0.0 collective-permute-done.down_ref
  35.4 0.0 collective-permute-done.1.up_ref
  35.4 2.5 %all-to-all-done.recv_ref = f32[32,9,2,128]{3,2,1,0:T(2,128)S(1)} async-done(((f32[32,9,2,128]{3,2,1,0:T(2,128)}), f32[32,9,2,128]{3,2,1,0:T(2,128)S(1)}, u32[]{:S(2)}, u32[]{:S(2)}) %all-to-all-start) | async-done | bytes 294944 | tf_op jit(solution)/shard_map/all_to_all | solution.py:314
  37.9 0.0 copy-done.2
  37.9 2.6 %finish.1 = (f32[6,128,128]{2,1,0:T(8,128)}, f32[3,512]{1,0:T(4,128)}) custom-call(f32[32,9,2,128]{3,2,1,0:T(2,128)S(1)} %all-to-all-done.recv_ref, f32[6,128]{1,0:T(8,128)S(1)} %collective-permute-done.down_ref, f32[6,128]{1,0:T(8,128)S(1)} %collective-permute-done.1.up_ref, s32[32,128]{1,0:T(8,128)S(1)} %bitcast.10, ...), custom_call_target="tpu_custom_call" | custom-call | tf_op jit(solution)/shard_map/finish/pallas_call | solution.py:331
Async XLA Ops:
  0.6 31.7 %copy-start.1 = (f32[1,32,128]{2,1,0:T(8,128)S(1)}, f32[1,32,128]{2,1,0:T(8,128)}, u32[]{:S(2)}) copy-start(f32[1,32,128]{2,1,0:T(8,128)} %param.16) | copy-start | bytes 49156
  0.6 31.7 %copy-start.5 = (s32[1,32]{1,0:T(1,128)S(1)}, s32[1,32]{1,0:T(1,128)}, u32[]{:S(2)}) copy-start(s32[1,32]{1,0:T(1,128)} %count_ref.1) | copy-start | bytes 388
  0.7 37.2 %copy-start.2 = (s32[1,32,128]{2,1,0:T(8,128)S(1)}, s32[1,32,128]{2,1,0:T(8,128)}, u32[]{:S(2)}) copy-start(s32[1,32,128]{2,1,0:T(8,128)} %param.15) | copy-start | bytes 49156
  19.2 18.7 %all-to-all-start = ((f32[32,9,2,128]{3,2,1,0:T(2,128)}), f32[32,9,2,128]{3,2,1,0:T(2,128)S(1)}, u32[]{:S(2)}, u32[]{:S(2)}) async-start(f32[32,9,2,128]{3,2,1,0:T(2,128)} %get-tuple-element.12), calls=%async_computation | async-start | bytes 589824 | tf_op jit(solution)/shard_map/all_to_all | solution.py:314
  26.5 8.9 %collective-permute-start = (f32[6,128]{1,0:T(8,128)}, f32[6,128]{1,0:T(8,128)S(1)}, u32[]{:S(2)}, u32[]{:S(2)}) collective-permute-start(f32[6,128]{1,0:T(8,128)} %get-tuple-element.13), channel_id=1, source_target_pairs={{4,0},{8,4},{12,8},{16,12},{20,16},{24,20},{28,24},{5,1},{9,5},{13... | collective-permute-start | bytes 9224 | tf_op jit(solution)/shard_map/ppermute | solution.py:25
  27.8 7.6 %collective-permute-start.1 = (f32[6,128]{1,0:T(8,128)}, f32[6,128]{1,0:T(8,128)S(1)}, u32[]{:S(2)}, u32[]{:S(2)}) collective-permute-start(f32[6,128]{1,0:T(8,128)} %get-tuple-element.14), channel_id=1, source_target_pairs={{0,4},{4,8},{8,12},{12,16},{16,20},{20,24},{24,28},{1,5},{5,9},{9,... | collective-permute-start | bytes 9224 | tf_op jit(solution)/shard_map/ppermute | solution.py:25
  32.4 1.0 %copy-start = (f32[6,128,128]{2,1,0:T(8,128)S(1)}, f32[6,128,128]{2,1,0:T(8,128)}, u32[]{:S(2)}) copy-start(f32[6,128,128]{2,1,0:T(8,128)} %get-tuple-element.15.base_ref) | copy-start | bytes 1179652
  33.4 0.7 %copy-start.3 = (f32[4,8,128]{2,1,0:T(8,128)S(1)}, f32[4,8,128]{2,1,0:T(8,128)}, u32[]{:S(2)}) copy-start(f32[4,8,128]{2,1,0:T(8,128)} %get-tuple-element.16.edge_down) | copy-start | bytes 49156
  34.1 0.7 %copy-start.4 = (f32[4,8,128]{2,1,0:T(8,128)S(1)}, f32[4,8,128]{2,1,0:T(8,128)}, u32[]{:S(2)}) copy-start(f32[4,8,128]{2,1,0:T(8,128)} %get-tuple-element.17.edge_up) | copy-start | bytes 49156

commit v6 on v4

--- a/solution.py
+++ b/solution.py
@@ -80,15 +80,17 @@
 
     def copies(step):
         at = pl.ds(pl.multiple_of(step * rows, rows), rows)
-        return (
-            pltpu.make_async_copy(metric_hbm.at[:, :, :, at, :], metric_part.at[step], metric_sem.at[step]),
-            pltpu.make_async_copy(diag_hbm.at[:, :, at, :], diag_part.at[step], diag_sem.at[step]),
-            pltpu.make_async_copy(face_hbm.at[:, :, :, at, :], face_part.at[step], face_sem.at[step]),
-        )
-
-    for step in range(steps):
-        for copy in copies(step):
-            copy.start()
+        found = []
+        for i in range(variables):
+            found += [
+                pltpu.make_async_copy(metric_hbm.at[i, :, :, at, :], metric_part.at[step, i], metric_sem.at[step, i]),
+                pltpu.make_async_copy(diag_hbm.at[i, :, at, :], diag_part.at[step, i], diag_sem.at[step, i]),
+                pltpu.make_async_copy(face_hbm.at[i, :, :, at, :], face_part.at[step, i], face_sem.at[step, i]),
+            ]
+        return found
+
+    for copy in copies(0):
+        copy.start()
 
     for i in range(variables):
         for half in range(span_rows):
@@ -125,6 +127,11 @@
     lane_ids = lax.broadcasted_iota(jnp.int32, (rows, width), 1)
 
     def cells(step, none):
+        @pl.when(step + 1 < steps)
+        def _():
+            for copy in copies(step + 1):
+                copy.start()
+
         for copy in copies(step):
             copy.wait()
         here = pl.ds(pl.multiple_of(step * rows, rows), rows)
@@ -295,9 +302,9 @@
             pltpu.VMEM((steps, variables, faces, variables, rows, width), jnp.float32),
             pltpu.VMEM((steps, 8, width), jnp.float32),
             pltpu.VMEM((steps, 8, width), jnp.float32),
-            pltpu.SemaphoreType.DMA((steps,)),
-            pltpu.SemaphoreType.DMA((steps,)),
-            pltpu.SemaphoreType.DMA((steps,)),
+            pltpu.SemaphoreType.DMA((steps, variables)),
+            pltpu.SemaphoreType.DMA((steps, variables)),
+            pltpu.SemaphoreType.DMA((steps, variables)),
         ],
         compiler_params=pltpu.CompilerParams(vmem_limit_bytes=VMEM_BYTES),
         cost_estimate=pl.CostEstimate(

time: 40.6 us -> 41.3 us (1.017)
  Pallas kernels: 21.5 us -> 22.3 us
    pallas_call x1, Pallas kernels: 18.4 us -> 19.1 us  [local(): pl.pallas_call(cells_and_nodes, in_specs=[vmem] * 3 + [hbm] * 3, out_spec...]
where the time goes in v6:
time: 41.3 us; the launch traced here: 41.1 us
  Pallas kernels  22.3 us (54%)
  starting transfers between devices  13.1 us (32%)
  waiting for transfers between devices  3.92 us (9%)
  local copies, waits for them, and re-layouts  1 us (2%)
  between operations  0.74 us (2%)
    pallas_call x1, Pallas kernels, local(): pl.pallas_call(cells_and_nodes, in_specs=[vmem] * 3 + [hbm] * 3, out_spec...  19.1 us
    all_to_all x1, starting transfers between devices, local(): lax.all_to_all(sent, ('dom', 'grid'), split_axis=0, concat_axis=0, tiled=...  7.3 us
    ppermute x2, starting transfers between devices, shifted(): return lax.ppermute(block, axis, route)  5.84 us
    all_to_all x1, waiting for transfers between devices, local(): lax.all_to_all(sent, ('dom', 'grid'), split_axis=0, concat_axis=0, tiled=...  3.91 us
    pallas_call x1, Pallas kernels, local(): pl.pallas_call(finish, in_specs=[vmem] * 6, out_specs=[vmem] * 2, out_sha...  2.62 us
    unnamed x8, local copies, waits for them, and re-layouts  1 us
  transfers between devices with their start and end apart: 3, of which 1 were waited for; matrix products, arithmetic and copies ran while one was open for 0% of the time, Pallas kernels for 1%

profile of v6, /device:TPU:0, one launch (start us, length us, event | category | flops | bytes accessed | tf_op | source)
XLA Modules:
  0.0 41.1 jit_solution(4181733386493016363)
XLA Ops:
  0.6 0.0 copy-start.1
  0.6 0.0 copy-start.3
  0.7 0.0 copy-start.2
  0.7 19.1 %cells_and_nodes.1 = (f32[32,9,2,128]{3,2,1,0:T(2,128)}, f32[6,128]{1,0:T(8,128)}, f32[6,128]{1,0:T(8,128)}, f32[6,128,128]{2,1,0:T(8,128)}) custom-call(f32[6,128,128]{2,1,0:T(8,128)} %bitcast.14, s32[32,128]{1,0:T(8,128)} %bitcast.17, s32[4,128,128]{2,1,0:T(8,128)} %bitcast.16, f32[6,3,4,128,128]{4,3,2,1,0:T(8,128)} %bitcast.12, ...), custom_call_target="tpu_custom_call" | custom-call | flops 12884901888 | bytes 16515072 | tf_op jit(solution)/shard_map/cells_and_nodes/pallas_call | solution.py:287
  19.7 7.3 %all-to-all-start = ((f32[32,9,2,128]{3,2,1,0:T(2,128)}), f32[32,9,2,128]{3,2,1,0:T(2,128)S(1)}, u32[]{:S(2)}, u32[]{:S(2)}) async-start(f32[32,9,2,128]{3,2,1,0:T(2,128)} %get-tuple-element.10), calls=%async_computation | async-start | bytes 589824 | tf_op jit(solution)/shard_map/all_to_all | solution.py:318
  27.0 1.3 %collective-permute-start = (f32[6,128]{1,0:T(8,128)}, f32[6,128]{1,0:T(8,128)S(1)}, u32[]{:S(2)}, u32[]{:S(2)}) collective-permute-start(f32[6,128]{1,0:T(8,128)} %get-tuple-element.11), channel_id=1, source_target_pairs={{4,0},{8,4},{12,8},{16,12},{20,16},{24,20},{28,24},{5,1},{9,5},{13... | collective-permute-start | bytes 9224 | tf_op jit(solution)/shard_map/ppermute | solution.py:25
  28.3 4.5 %collective-permute-start.1 = (f32[6,128]{1,0:T(8,128)}, f32[6,128]{1,0:T(8,128)S(1)}, u32[]{:S(2)}, u32[]{:S(2)}) collective-permute-start(f32[6,128]{1,0:T(8,128)} %get-tuple-element.12), channel_id=1, source_target_pairs={{0,4},{4,8},{8,12},{12,16},{16,20},{20,24},{24,28},{1,5},{5,9},{9,... | collective-permute-start | bytes 9224 | tf_op jit(solution)/shard_map/ppermute | solution.py:25
  32.9 0.0 copy-done.1
  32.9 0.0 copy-done.3
  32.9 0.0 copy-start
  32.9 1.0 %copy-done = f32[6,128,128]{2,1,0:T(8,128)S(1)} copy-done((f32[6,128,128]{2,1,0:T(8,128)S(1)}, f32[6,128,128]{2,1,0:T(8,128)}, u32[]{:S(2)}) %copy-start) | copy-done | bytes 393240
  33.9 0.6 %prepare.1 = (f32[32,128]{1,0:T(8,128)S(1)}, f32[6,128,128]{2,1,0:T(8,128)S(1)}) custom-call(s32[1,32]{1,0:T(1,128)S(1)} %copy-done.3, f32[32,128]{1,0:T(8,128)S(1)} %bitcast.9, f32[6,128,128]{2,1,0:T(8,128)S(1)} %copy-done), custom_call_target="tpu_custom_call" | custom-call | flops 98304 | bytes 786432 | tf_op jit(solution)/shard_map/prepare/pallas_call | solution.py:322
  34.5 0.0 collective-permute-done.down_ref
  34.5 0.0 collective-permute-done.1.up_ref
  34.5 3.9 %all-to-all-done.recv_ref = f32[32,9,2,128]{3,2,1,0:T(2,128)S(1)} async-done(((f32[32,9,2,128]{3,2,1,0:T(2,128)}), f32[32,9,2,128]{3,2,1,0:T(2,128)S(1)}, u32[]{:S(2)}, u32[]{:S(2)}) %all-to-all-start) | async-done | bytes 294944 | tf_op jit(solution)/shard_map/all_to_all | solution.py:318
  38.4 0.0 copy-done.2
  38.4 2.6 %finish.1 = (f32[6,128,128]{2,1,0:T(8,128)}, f32[3,512]{1,0:T(4,128)}) custom-call(f32[32,9,2,128]{3,2,1,0:T(2,128)S(1)} %all-to-all-done.recv_ref, f32[6,128]{1,0:T(8,128)S(1)} %collective-permute-done.down_ref, f32[6,128]{1,0:T(8,128)S(1)} %collective-permute-done.1.up_ref, s32[32,128]{1,0:T(8,128)S(1)} %bitcast.10, ...), custom_call_target="tpu_custom_call" | custom-call | tf_op jit(solution)/shard_map/finish/pallas_call | solution.py:335
Async XLA Ops:
  0.6 32.3 %copy-start.1 = (f32[1,32,128]{2,1,0:T(8,128)S(1)}, f32[1,32,128]{2,1,0:T(8,128)}, u32[]{:S(2)}) copy-start(f32[1,32,128]{2,1,0:T(8,128)} %param.16) | copy-start | bytes 49156
  0.6 32.3 %copy-start.3 = (s32[1,32]{1,0:T(1,128)S(1)}, s32[1,32]{1,0:T(1,128)}, u32[]{:S(2)}) copy-start(s32[1,32]{1,0:T(1,128)} %count_ref.1) | copy-start | bytes 388
  0.7 37.8 %copy-start.2 = (s32[1,32,128]{2,1,0:T(8,128)S(1)}, s32[1,32,128]{2,1,0:T(8,128)}, u32[]{:S(2)}) copy-start(s32[1,32,128]{2,1,0:T(8,128)} %param.15) | copy-start | bytes 49156
  19.7 18.7 %all-to-all-start = ((f32[32,9,2,128]{3,2,1,0:T(2,128)}), f32[32,9,2,128]{3,2,1,0:T(2,128)S(1)}, u32[]{:S(2)}, u32[]{:S(2)}) async-start(f32[32,9,2,128]{3,2,1,0:T(2,128)} %get-tuple-element.10), calls=%async_computation | async-start | bytes 589824 | tf_op jit(solution)/shard_map/all_to_all | solution.py:318
  27.0 7.5 %collective-permute-start = (f32[6,128]{1,0:T(8,128)}, f32[6,128]{1,0:T(8,128)S(1)}, u32[]{:S(2)}, u32[]{:S(2)}) collective-permute-start(f32[6,128]{1,0:T(8,128)} %get-tuple-element.11), channel_id=1, source_target_pairs={{4,0},{8,4},{12,8},{16,12},{20,16},{24,20},{28,24},{5,1},{9,5},{13... | collective-permute-start | bytes 9224 | tf_op jit(solution)/shard_map/ppermute | solution.py:25
  28.3 6.2 %collective-permute-start.1 = (f32[6,128]{1,0:T(8,128)}, f32[6,128]{1,0:T(8,128)S(1)}, u32[]{:S(2)}, u32[]{:S(2)}) collective-permute-start(f32[6,128]{1,0:T(8,128)} %get-tuple-element.12), channel_id=1, source_target_pairs={{0,4},{4,8},{8,12},{12,16},{16,20},{20,24},{24,28},{1,5},{5,9},{9,... | collective-permute-start | bytes 9224 | tf_op jit(solution)/shard_map/ppermute | solution.py:25
  32.9 1.0 %copy-start = (f32[6,128,128]{2,1,0:T(8,128)S(1)}, f32[6,128,128]{2,1,0:T(8,128)}, u32[]{:S(2)}) copy-start(f32[6,128,128]{2,1,0:T(8,128)} %get-tuple-element.13.base_ref) | copy-start | bytes 1179652
